TPU v7x, 32 devices: a whole 2x2x4 slice. The times are simulated.
32 devices in a mesh: grp: 4 (over x, core), dev: 8 (over z, y).
Axes of the slice: x: 2, y: 2, z: 4, core: 2. Of those that a mesh axis runs over, the one named last changes fastest.
Arguments:
- solid_mask: int32 [96, 256, 128], P('grp', 'dev'), may hold values 0 or 1
- forcing: float32 [3, 96, 256, 128], P(None, 'grp', 'dev'), may hold values from -18 to 18
Outputs:
- velocity: float32 [3, 96, 256, 128], P(None, 'grp', 'dev')
- pressure: float32 [96, 256, 128], P('grp', 'dev')
All inputs are finite; a program needn't handle non-finite values. No bound on the sum of `solid_mask` on one device may be relied on, other than what follows from the above.
Results may differ from a plain program's by a relative error of at most 0.000073.
Values sent between devices are 32-bit elements; how exact they have to be, the bound alone decides.
No kernel may reach another device: no remote copies, remote signals or barrier semaphores. Data moves between devices by JAX's collectives and lax.ppermute only.
A program may use at most 192 MiB of HBM per device.

v0:
```python
import jax
import jax.numpy as jnp
from jax import lax
from jax.sharding import PartitionSpec as P

viscosity = 1.0
penalty = 10.0
relaxation = 0.8
pressure_step = 1.0
mean_drive = 1.0


def with_halo(cells, sides, width):
    for axis, dim in sides:
        count = lax.axis_size(axis)
        head = lax.slice_in_dim(cells, 0, width, axis=dim)
        tail = lax.slice_in_dim(cells, cells.shape[dim] - width, cells.shape[dim], axis=dim)
        cells = jnp.concatenate(
            [
                lax.ppermute(tail, axis, [(i, (i + 1) % count) for i in range(count)]),
                cells,
                lax.ppermute(head, axis, [((i + 1) % count, i) for i in range(count)]),
            ],
            axis=dim,
        )
    return cells


def trim_plane(field, width):
    return field[..., width : field.shape[-3] - width, width : field.shape[-2] - width, :]


def laplace(field, spacing):
    middle = trim_plane(field, 1)
    summed = (
        field[..., 2:, 1:-1, :]
        + field[..., :-2, 1:-1, :]
        + field[..., 1:-1, 2:, :]
        + field[..., 1:-1, :-2, :]
    )
    summed = summed + jnp.roll(middle, 1, -1) + jnp.roll(middle, -1, -1) - 6.0 * middle
    return summed / (spacing * spacing)


def gradient(field, spacing):
    middle = trim_plane(field, 1)
    along_x = field[2:, 1:-1, :] - field[:-2, 1:-1, :]
    along_y = field[1:-1, 2:, :] - field[1:-1, :-2, :]
    along_z = jnp.roll(middle, -1, -1) - jnp.roll(middle, 1, -1)
    return jnp.stack([along_x, along_y, along_z]) / (2.0 * spacing)


def divergence(field, spacing):
    middle = field[2, 1:-1, 1:-1, :]
    summed = (
        field[0, 2:, 1:-1, :]
        - field[0, :-2, 1:-1, :]
        + (field[1, 1:-1, 2:, :] - field[1, 1:-1, :-2, :])
    )
    summed = summed + (jnp.roll(middle, -1, -1) - jnp.roll(middle, 1, -1))
    return summed / (2.0 * spacing)


def velocity_update(velo_rim, press_rim, solid_share, force_part, spacing):
    middle = trim_plane(velo_rim, 1)
    damping = penalty * solid_share
    diagonal = 6.0 * viscosity / (spacing * spacing) + damping
    residual = (
        force_part
        - gradient(press_rim, spacing)
        + viscosity * laplace(velo_rim, spacing)
        - damping * middle
    )
    return middle + relaxation * residual / diagonal


def block_mean(field):
    leading = field.shape[:-3]
    sizes_a, sizes_b, sizes_c = field.shape[-3:]
    shaped = field.reshape(leading + (sizes_a // 4, 4, sizes_b // 4, 4, sizes_c // 4, 4))
    return shaped.mean(axis=(-5, -3, -1))


def interpolation(fine_len, coarse_len, period):
    fine_rows = lax.broadcasted_iota(jnp.int32, (fine_len, coarse_len), 0)
    coarse_cols = lax.broadcasted_iota(jnp.int32, (fine_len, coarse_len), 1)
    lower_index = (fine_rows - 2) // 4
    fraction = ((fine_rows + 2) % 4).astype(jnp.float32) * 0.25 + 0.125
    first_hit = (lower_index - coarse_cols) % period == 0
    second_hit = (lower_index + 1 - coarse_cols) % period == 0
    return jnp.where(first_hit, 1.0 - fraction, 0.0) + jnp.where(second_hit, fraction, 0.0)


def expand_axis(field, axis, fine_len, coarse_rim, extension):
    repeated = jnp.repeat(field, 4, axis=axis)
    start = 4 * coarse_rim - 2 - extension
    length = fine_len + 2 * extension
    lower = lax.slice_in_dim(repeated, start, start + length, axis=axis)
    upper = lax.slice_in_dim(repeated, start + 4, start + 4 + length, axis=axis)
    positions = lax.iota(jnp.int32, length) - extension
    fraction = ((positions + 2) % 4).astype(jnp.float32) * 0.25 + 0.125
    shape = [1] * field.ndim
    shape[axis] = length
    fraction = fraction.reshape(shape)
    return (1.0 - fraction) * lower + fraction * upper


def local_sweeps(velo_now, press_now, solid_share, force_part, spacing):
    for number in range(2):
        solid_share = trim_plane(solid_share, 1)
        force_part = trim_plane(force_part, 1)
        new_velocity = velocity_update(velo_now, press_now, solid_share, force_part, spacing)
        press_now = trim_plane(press_now, 2) - pressure_step * divergence(new_velocity, spacing)
        velo_now = trim_plane(new_velocity, 1)
        solid_share = trim_plane(solid_share, 1)
        force_part = trim_plane(force_part, 1)
    return (velo_now, press_now)


def shards(solid_mask, forcing):
    solid_share = solid_mask.astype(jnp.float32)
    drive_vector = jnp.array([mean_drive, 0.0, 0.0], dtype=jnp.float32).reshape(3, 1, 1, 1)
    force_all = forcing + drive_vector
    coarse_local = jnp.concatenate([block_mean(solid_share)[None], block_mean(force_all)], 0)
    extension = 0
    coarse_rim = 1 + extension // 4
    margin = 4 + coarse_rim
    coarse_z = coarse_local.shape[3]
    widened = with_halo(coarse_local, (("grp", 1),), margin)
    padded = with_halo(widened, (("dev", 2),), margin)
    zero_velocity = jnp.zeros((3,) + padded.shape[1:], jnp.float32)
    zero_pressure = jnp.zeros(padded.shape[1:], jnp.float32)
    coarse_velocity, coarse_pressure = local_sweeps(
        zero_velocity, zero_pressure, padded[0], padded[1:], 4.0
    )
    stacked = jnp.concatenate([coarse_velocity, coarse_pressure[None]], 0)
    size_x, size_y, size_z = solid_mask.shape
    along_z = interpolation(size_z, coarse_z, coarse_z)
    stacked = jnp.einsum("fabk,zk->fabz", stacked, along_z, precision=lax.Precision.HIGHEST)
    stacked = expand_axis(stacked, 2, size_y, coarse_rim, extension)
    fine_state = expand_axis(stacked, 1, size_x, coarse_rim, extension)
    state_now = fine_state
    for number in range(2):
        rimmed_state = with_halo(state_now, (("grp", 1), ("dev", 2)), 1)
        new_velocity = velocity_update(
            rimmed_state[:3], rimmed_state[3], solid_share, force_all, 1.0
        )
        rimmed_velocity = with_halo(new_velocity, (("grp", 1), ("dev", 2)), 1)
        press_now = state_now[3] - pressure_step * divergence(rimmed_velocity, 1.0)
        velo_now = new_velocity
        if number == 0:
            state_now = jnp.concatenate([new_velocity, press_now[None]], 0)
    return (velo_now, press_now)


def solution(mesh):
    in_specs = (P("grp", "dev", None), P(None, "grp", "dev", None))
    out_specs = (P(None, "grp", "dev", None), P("grp", "dev", None))
    return jax.shard_map(shards, mesh=mesh, in_specs=in_specs, out_specs=out_specs, check_vma=False)
```

profile of v0, /device:TPU:0, one launch (start us, length us, event | category | flops | bytes accessed | tf_op | source)
XLA Modules:
  0.0 335.1 jit_solution(993642352080061627)
XLA Ops:
  1.7 4.4 %copy.188 = f32[3,24,32,128]{2,1,3,0:T(8,128)} copy(f32[3,24,32,128]{3,2,1,0:T(8,128)} %param.4) | data formatting | bytes 2359296 | tf_op args[1]
  6.1 4.9 %broadcast_add_fusion = f32[3,24,32,128]{2,1,3,0:T(8,128)} fusion(f32[3,24,32,128]{2,1,3,0:T(8,128)} %copy.188, f32[3]{0:T(128)S(1)} %copy-done.13), kind=kLoop, calls=%fused_computation.39 | loop fusion | flops 294912 | bytes 2359308 | tf_op jit(solution)/shard_map/add | solution.py:123
  11.0 3.7 %copy.189 = f32[3,24,32,128]{3,2,1,0:T(8,128)S(1)} copy(f32[3,24,32,128]{2,1,3,0:T(8,128)} %broadcast_add_fusion) | data formatting | bytes 2359296 | tf_op jit(solution)/shard_map/add | solution.py:123
  14.7 14.4 %reshape.313 = f32[6,4,8,4,32,4]{5,4,3,2,1,0:T(8,128)} reshape(f32[24,32,128]{2,1,0:T(8,128)S(1)} %convert_element_type.32) | data formatting | bytes 786432 | tf_op jit(solution)/shard_map/reshape | solution.py:80
  29.1 5.6 %reduce_sum.18 = f32[6,8,32]{2,1,0:T(8,128)S(1)} reduce(f32[6,4,8,4,32,4]{5,4,3,2,1,0:T(8,128)} %reshape.313, f32[]{:T(128)} %constant.125.clone.1), dimensions={1,3,5}, to_apply=%region_0.0 | reduce | flops 96768 | bytes 399364 | tf_op jit(solution)/shard_map/reduce_sum | solution.py:81
  34.7 40.3 %reshape.314 = f32[3,6,4,8,4,32,4]{6,5,4,3,2,1,0:T(8,128)} reshape(f32[3,24,32,128]{3,2,1,0:T(8,128)S(1)} %copy.189) | data formatting | bytes 2359296 | tf_op jit(solution)/shard_map/reshape | solution.py:80
  74.9 14.0 %reduce_sum.19 = f32[3,6,8,32]{3,2,1,0:T(8,128)S(1)} reduce(f32[3,6,4,8,4,32,4]{6,5,4,3,2,1,0:T(8,128)} %reshape.314, f32[]{:T(128)} %constant.125.clone.1), dimensions={2,4,6}, to_apply=%region_1.0 | reduce | flops 290304 | bytes 1198084 | tf_op jit(solution)/shard_map/reduce_sum | solution.py:81
  89.5 2.0 collective-permute-start.1
  91.6 1.9 collective-permute-done
  95.1 1.6 collective-permute-start.2
  96.7 3.2 collective-permute-start.3
  100.5 1.6 copy.201
  102.2 6.6 %collective-permute-done.2 = f32[4,16,5,32]{3,2,1,0:T(8,128)S(1)} collective-permute-done((f32[4,16,5,32]{3,2,1,0:T(8,128)}, f32[4,16,5,32]{3,2,1,0:T(8,128)S(1)}, u32[]{:S(2)}, u32[]{:S(2)}) %collective-permute-start.2) | collective-permute-done | bytes 40992 | tf_op jit(solution)/shard_map/ppermute | solution.py:20
  108.8 2.8 collective-permute-done.3
  114.2 1.9 copy.193
  116.1 7.3 %broadcast_in_dim.14 = f32[4,8,4,32,128]{3,2,1,4,0:T(4,128)} broadcast(f32[4,8,32,128]{2,1,3,0:T(8,128)} %copy.193), dimensions={0,1,3,4} | broadcast | bytes 2621440 | tf_op jit(solution)/shard_map/broadcast_in_dim | solution.py:95
  123.4 7.7 %fusion = f32[4,24,32,128]{2,1,3,0:T(8,128)S(1)} fusion(f32[4,32,32,128]{2,1,3,0:T(8,128)} %bitcast.109, f32[24]{0:T(128)S(1)} %get-tuple-element.106, f32[24]{0:T(128)S(1)} %get-tuple-element.107), kind=kLoop, calls=%fused_computation.2 | loop fusion | flops 1179648 | bytes 4718784 | tf_op jit(solution)/shard_map/add | solution.py:105
  131.7 1.6 collective-permute-start.5
  133.4 4.3 %fusion.130 = (f32[3,24,32,127]{2,1,3,0:T(8,128)}, f32[3,24,32,127]{2,1,3,0:T(8,128)}) fusion(f32[4,24,32,128]{2,1,3,0:T(8,128)S(1)} %fusion), kind=kLoop, calls=%fused_computation.268 | loop fusion | bytes 4681728 | tf_op jit(solution)/shard_map/jit(_roll_static)/slice | solution.py:41
  139.0 1.8 pad_maximum_fusion
  140.8 7.3 %fusion.129 = (f32[4,26,1,128]{2,1,3,0:T(8,128)}, f32[4,26,1,128]{2,1,3,0:T(8,128)}) fusion(f32[4,26,32,128]{2,1,3,0:T(8,128)S(1)} %pad_maximum_fusion), kind=kLoop, calls=%fused_computation.267 | loop fusion | bytes 212992 | tf_op jit(solution)/shard_map/slice | solution.py:16
  148.1 5.2 %copy.195 = f32[4,26,1,128]{3,0,2,1:T(4,128)S(1)} copy(f32[4,26,1,128]{2,1,3,0:T(8,128)} %get-tuple-element.14) | data formatting | bytes 106496 | tf_op jit(solution)/shard_map/slice | solution.py:16
  153.3 5.2 %copy.194 = f32[4,26,1,128]{3,0,2,1:T(4,128)S(1)} copy(f32[4,26,1,128]{2,1,3,0:T(8,128)} %get-tuple-element.15) | data formatting | bytes 106496 | tf_op jit(solution)/shard_map/slice | solution.py:17
  158.8 4.8 %collective-permute-start.7 = (f32[4,26,1,128]{3,0,2,1:T(4,128)S(1)}, f32[4,26,1,128]{3,0,2,1:T(4,128)S(1)}, u32[]{:S(2)}, u32[]{:S(2)}) collective-permute-start(f32[4,26,1,128]{3,0,2,1:T(4,128)S(1)} %copy.195), channel_id=1, source_target_pairs={{1,0},{2,1},{3,2},{4,3},{5,4},{6,5},{7,6},{0,7},{9,8},{10,9},{11,1... | collective-permute-start | bytes 159752 | tf_op jit(solution)/shard_map/ppermute | solution.py:22
  164.3 1.3 collective-permute-done.7
  165.6 4.7 %copy.197 = f32[4,26,1,128]{2,1,3,0:T(8,128)} copy(f32[4,26,1,128]{3,0,2,1:T(4,128)S(1)} %collective-permute-done.7) | data formatting | bytes 106496 | tf_op jit(solution)/shard_map/ppermute | solution.py:22
  170.3 5.0 %copy.196 = f32[4,26,1,128]{2,1,3,0:T(8,128)} copy(f32[4,26,1,128]{3,0,2,1:T(4,128)S(1)} %collective-permute-done.6) | data formatting | bytes 106496 | tf_op jit(solution)/shard_map/ppermute | solution.py:20
  175.3 4.1 %fusion.25 = f32[26,34,128]{1,0,2:T(8,128)S(1)} fusion(f32[4,26,1,128]{2,1,3,0:T(8,128)} %copy.197, f32[4,26,1,128]{2,1,3,0:T(8,128)} %copy.196, f32[4,1,32,128]{2,1,3,0:T(1,128)S(1)} %collective-permute-done.5, f32[4,24,32,128]{2,1,3,0:T(8,128)} %copy-done, f32[4,1,32,128]{2,1,3,0:T(1,128)S(1)} %collective-permute-done.4), kind=kLoop, calls=%fused_computation.44 | loop fusion | flops 452608 | bytes 2263040 | tf_op jit(solution)/shard_map/squeeze | solution.py:146
  180.4 3.0 fusion.37
  183.4 1.3 maximum_subtract_fusion
  186.8 13.8 %fusion.19 = f32[3,24,32,128]{2,1,3,0:T(8,128)S(1)} fusion(f32[4,26,1,128]{2,1,3,0:T(8,128)} %copy.196, f32[4,1,32,128]{2,1,3,0:T(1,128)} %copy-done.6, f32[4,24,32,128]{2,1,3,0:T(8,128)S(1)} %bitcast.102, f32[4,1,32,128]{2,1,3,0:T(1,128)S(1)} %collective-permute-done.4, f32[4,26,1,128]{2,1,3,0:T(8,128)} %copy.197, ...), kind=kLoop, calls=%fused_computation.25 | loop fusion | flops 8257536 | bytes 26414592 | tf_op jit(solution)/shard_map/add | solution.py:74
  201.9 4.2 %fusion.134 = (f32[3,24,32,127]{2,1,3,0:T(8,128)}, f32[3,24,32,127]{2,1,3,0:T(8,128)}) fusion(f32[3,24,32,128]{2,1,3,0:T(8,128)S(1)} %fusion.19), kind=kLoop, calls=%fused_computation.272 | loop fusion | bytes 4681728 | tf_op jit(solution)/shard_map/jit(_roll_static)/slice | solution.py:41
  206.1 1.7 collective-permute-start.8
  207.9 2.8 fusion.141
  210.7 3.7 %copy.207 = f32[3,24,32,128]{3,2,1,0:T(8,128)S(1)} copy(f32[3,24,32,128]{2,1,3,0:T(8,128)} %copy-done.1) | data formatting | bytes 2359296 | tf_op jit(solution)/shard_map/add | solution.py:74
  214.7 1.2 collective-permute-start.11
  215.9 4.1 %collective-permute-start.10 = (f32[3,26,1,128]{3,2,1,0:T(1,128)S(1)}, f32[3,26,1,128]{3,2,1,0:T(1,128)S(1)}, u32[]{:S(2)}, u32[]{:S(2)}) collective-permute-start(f32[3,26,1,128]{3,2,1,0:T(1,128)S(1)} %get-tuple-element.67), channel_id=1, source_target_pairs={{1,0},{2,1},{3,2},{4,3},{5,4},{6,5},{7,6},{0,7},{9,8},{10,9},{11,1... | collective-permute-start | bytes 119816 | tf_op jit(solution)/shard_map/ppermute | solution.py:22
  220.0 1.3 fusion.140
  222.7 2.7 copy.231
  225.4 1.7 copy.230
  227.0 6.9 %fusion.40 = (f32[1,24,32,128]{2,1,3,0:T(8,128)}, f32[1,24,32,128]{2,1,3,0:T(8,128)}) fusion(f32[1,24,32,1]{2,1,3,0:T(8,128)S(1)} %get-tuple-element.49, f32[1,24,32,127]{2,1,3,0:T(8,128)} %get-tuple-element.53, f32[1,24,32,127]{2,1,3,0:T(8,128)} %get-tuple-element.54, f32[1,24,32,1]{2,1,3,0:T(8,128)S(1)} %get-tuple-element.50, ...), kind=kLoop, calls=%fused_computation.75 | loop fusion | flops 1081344 | bytes 4030464 | tf_op jit(solution)/shard_map/sub | solution.py:149
  233.9 1.8 copy.208
  235.9 1.7 collective-permute-start.13
  241.7 5.2 %collective-permute-start.15 = (f32[4,26,1,128]{3,0,2,1:T(4,128)}, f32[4,26,1,128]{3,0,2,1:T(4,128)S(1)}, u32[]{:S(2)}, u32[]{:S(2)}) collective-permute-start(f32[4,26,1,128]{3,0,2,1:T(4,128)} %copy.233), channel_id=1, source_target_pairs={{1,0},{2,1},{3,2},{4,3},{5,4},{6,5},{7,6},{0,7},{9,8},{10,9},{11,1... | collective-permute-start | bytes 159752 | tf_op jit(solution)/shard_map/ppermute | solution.py:22
  246.9 1.7 pad_maximum_fusion.22
  248.6 8.4 %copy.212 = f32[4,26,32,128]{2,1,3,0:T(8,128)} copy(f32[4,26,32,128]{3,2,1,0:T(8,128)} %copy-done.4) | data formatting | bytes 3407872 | tf_op jit(solution)/shard_map/concatenate | solution.py:18
  257.0 4.5 %copy.235 = f32[3,24,32,128]{2,1,3,0:T(8,128)} copy(f32[3,24,32,128]{3,2,1,0:T(8,128)} %get-tuple-element.56) | data formatting | bytes 2359296
  261.5 3.3 copy.234
  264.8 4.9 %copy.213 = f32[4,26,1,128]{2,1,3,0:T(8,128)} copy(f32[4,26,1,128]{3,0,2,1:T(4,128)S(1)} %collective-permute-done.15) | data formatting | bytes 106496 | tf_op jit(solution)/shard_map/ppermute | solution.py:22
  269.7 4.8 %copy.211 = f32[4,26,1,128]{2,1,3,0:T(8,128)} copy(f32[4,26,1,128]{3,0,2,1:T(4,128)S(1)} %collective-permute-done.14) | data formatting | bytes 106496 | tf_op jit(solution)/shard_map/ppermute | solution.py:20
  274.5 4.0 %fusion.24 = f32[26,34,128]{1,0,2:T(8,128)S(1)} fusion(f32[4,26,1,128]{2,1,3,0:T(8,128)} %copy.213, f32[4,26,32,128]{2,1,3,0:T(8,128)} %copy.212, f32[4,26,1,128]{2,1,3,0:T(8,128)} %copy.211), kind=kLoop, calls=%fused_computation.41 | loop fusion | flops 226304 | bytes 2263040 | tf_op jit(solution)/shard_map/squeeze | solution.py:146
  279.5 2.9 fusion.33
  282.4 1.5 maximum_subtract_fusion.2
  283.9 20.5 %fusion.9 = f32[3,24,32,128]{2,1,3,0:T(8,128)} fusion(f32[3,24,32,128]{2,1,3,0:T(8,128)S(1)} %bitcast.104, f32[4,26,32,128]{2,1,3,0:T(8,128)} %copy.212, f32[4,26,1,128]{2,1,3,0:T(8,128)} %copy.211, f32[4,26,1,128]{2,1,3,0:T(8,128)} %copy.213, f32[1,24,32,128]{2,1,3,0:T(8,128)} %maximum_subtract_fusion.2, f32[1,24,32,128]{2,1,3,0:T(8,128)} %get-tuple-element.31, ...), kind=kLoop, calls=%fused_computation.13 | loop fusion | flops 6488064 | bytes 12034060 | tf_op jit(solution)/shard_map/add | solution.py:74
  304.4 2.8 fusion.133
  307.3 1.5 slice_bitcast_fusion
  308.8 1.5 collective-permute-start.16
  310.3 1.8 fusion.139
  312.1 3.7 %copy.225 = f32[3,24,32,128]{3,2,1,0:T(8,128)S(1)} copy(f32[3,24,32,128]{2,1,3,0:T(8,128)} %fusion.9) | data formatting | bytes 2359296
  315.9 1.5 collective-permute-done.17
  317.7 4.9 %collective-permute-start.18 = (f32[3,26,1,128]{3,2,1,0:T(1,128)S(1)}, f32[3,26,1,128]{3,2,1,0:T(1,128)S(1)}, u32[]{:S(2)}, u32[]{:S(2)}) collective-permute-start(f32[3,26,1,128]{3,2,1,0:T(1,128)S(1)} %get-tuple-element.63), channel_id=1, source_target_pairs={{1,0},{2,1},{3,2},{4,3},{5,4},{6,5},{7,6},{0,7},{9,8},{10,9},{11,1... | collective-permute-start | bytes 119816 | tf_op jit(solution)/shard_map/ppermute | solution.py:22
  323.2 1.2 collective-permute-done.19
  325.6 6.7 %fusion.31 = f32[24,32,128]{1,0,2:T(8,128)} fusion(f32[3,24,32,128]{2,1,3,0:T(8,128)} %fusion.9, f32[3,1,32,128]{2,1,3,0:T(1,128)} %copy-done.9, f32[3,1,32,128]{2,1,3,0:T(1,128)} %copy-done.8, f32[24,32,1]{1,0,2:T(8,128)} %get-tuple-element.51, f32[24,32,127]{1,0,2:T(8,128)} %get-tuple-element.55, f32[24,32,127]{1,0,2:T(8,128)} %get-tuple-element.52, ...), kind=kLoop, calls=%fused_computation.56 | loop fusion | flops 1671168 | bytes 4816896 | tf_op jit(solution)/shard_map/sub | solution.py:149
  332.3 2.6 copy.226
  (143 shorter events, 22.2 us)
Async XLA Ops:
  1.7 4.4 %copy-start.13 = (f32[3]{0:T(128)S(1)}, f32[3]{0:T(128)}, u32[]{:S(2)}) copy-start(f32[3]{0:T(128)} %constant.138.clone) | copy-start | bytes 40
  74.9 16.6 %copy-start.7 = (s32[24,32,128]{2,1,0:T(8,128)S(1)}, s32[24,32,128]{2,1,0:T(8,128)}, u32[]{:S(2)}) copy-start(s32[24,32,128]{2,1,0:T(8,128)} %param.3) | copy-start | bytes 1179652
  89.0 4.6 %collective-permute-start = (f32[4,5,8,32]{3,2,1,0:T(8,128)S(1)}, f32[4,5,8,32]{3,2,1,0:T(8,128)S(1)}, u32[]{:S(2)}, u32[]{:S(2)}) collective-permute-start(f32[4,5,8,32]{3,2,1,0:T(8,128)S(1)} %get-tuple-element.90), channel_id=1, source_target_pairs={{0,8},{8,16},{16,24},{24,0},{1,9},{9,17},{17,25},{25,1},{2,10},{10... | collective-permute-start | bytes 61448 | tf_op jit(solution)/shard_map/ppermute | solution.py:20
  89.5 4.7 %collective-permute-start.1 = (f32[4,5,8,32]{3,2,1,0:T(8,128)S(1)}, f32[4,5,8,32]{3,2,1,0:T(8,128)S(1)}, u32[]{:S(2)}, u32[]{:S(2)}) collective-permute-start(f32[4,5,8,32]{3,2,1,0:T(8,128)S(1)} %get-tuple-element.91), channel_id=1, source_target_pairs={{8,0},{16,8},{24,16},{0,24},{9,1},{17,9},{25,17},{1,25},{10,2},{18... | collective-permute-start | bytes 61448 | tf_op jit(solution)/shard_map/ppermute | solution.py:22
  95.1 13.7 %collective-permute-start.2 = (f32[4,16,5,32]{3,2,1,0:T(8,128)}, f32[4,16,5,32]{3,2,1,0:T(8,128)S(1)}, u32[]{:S(2)}, u32[]{:S(2)}) collective-permute-start(f32[4,16,5,32]{3,2,1,0:T(8,128)} %get-tuple-element.74), channel_id=1, source_target_pairs={{0,1},{1,2},{2,3},{3,4},{4,5},{5,6},{6,7},{7,0},{8,9},{9,10},{10,1... | collective-permute-start | bytes 122888 | tf_op jit(solution)/shard_map/ppermute | solution.py:20
  96.7 14.9 %collective-permute-start.3 = (f32[4,16,5,32]{3,2,1,0:T(8,128)}, f32[4,16,5,32]{3,2,1,0:T(8,128)S(1)}, u32[]{:S(2)}, u32[]{:S(2)}) collective-permute-start(f32[4,16,5,32]{3,2,1,0:T(8,128)} %get-tuple-element.75), channel_id=1, source_target_pairs={{1,0},{2,1},{3,2},{4,3},{5,4},{6,5},{7,6},{0,7},{9,8},{10,9},{11,1... | collective-permute-start | bytes 122888 | tf_op jit(solution)/shard_map/ppermute | solution.py:22
  131.2 7.8 %copy-start = (f32[4,24,32,128]{2,1,3,0:T(8,128)}, f32[4,24,32,128]{2,1,3,0:T(8,128)S(1)}, u32[]{:S(2)}) copy-start(f32[4,24,32,128]{2,1,3,0:T(8,128)S(1)} %fusion) | copy-start | bytes 4718596
  131.6 7.1 %collective-permute-start.4 = (f32[4,1,32,128]{2,1,3,0:T(1,128)S(1)}, f32[4,1,32,128]{2,1,3,0:T(1,128)S(1)}, u32[]{:S(2)}, u32[]{:S(2)}) collective-permute-start(f32[4,1,32,128]{2,1,3,0:T(1,128)S(1)} %get-tuple-element.20), channel_id=1, source_target_pairs={{0,8},{8,16},{16,24},{24,0},{1,9},{9,17},{17,25},{25,1},{2,10},{10... | collective-permute-start | bytes 196616 | tf_op jit(solution)/shard_map/ppermute | solution.py:20
  131.7 7.2 %collective-permute-start.5 = (f32[4,1,32,128]{2,1,3,0:T(1,128)S(1)}, f32[4,1,32,128]{2,1,3,0:T(1,128)S(1)}, u32[]{:S(2)}, u32[]{:S(2)}) collective-permute-start(f32[4,1,32,128]{2,1,3,0:T(1,128)S(1)} %get-tuple-element.21), channel_id=1, source_target_pairs={{8,0},{16,8},{24,16},{0,24},{9,1},{17,9},{25,17},{1,25},{10,2},{18... | collective-permute-start | bytes 196616 | tf_op jit(solution)/shard_map/ppermute | solution.py:22
  138.9 36.4 %copy-start.6 = (f32[4,1,32,128]{2,1,3,0:T(1,128)}, f32[4,1,32,128]{2,1,3,0:T(1,128)S(1)}, u32[]{:S(2)}) copy-start(f32[4,1,32,128]{2,1,3,0:T(1,128)S(1)} %collective-permute-done.5) | copy-start | bytes 196612
  158.6 11.8 %collective-permute-start.6 = (f32[4,26,1,128]{3,0,2,1:T(4,128)S(1)}, f32[4,26,1,128]{3,0,2,1:T(4,128)S(1)}, u32[]{:S(2)}, u32[]{:S(2)}) collective-permute-start(f32[4,26,1,128]{3,0,2,1:T(4,128)S(1)} %copy.194), channel_id=1, source_target_pairs={{0,1},{1,2},{2,3},{3,4},{4,5},{5,6},{6,7},{7,0},{8,9},{9,10},{10,1... | collective-permute-start | bytes 159752 | tf_op jit(solution)/shard_map/ppermute | solution.py:20
  158.8 6.9 %collective-permute-start.7 = (f32[4,26,1,128]{3,0,2,1:T(4,128)S(1)}, f32[4,26,1,128]{3,0,2,1:T(4,128)S(1)}, u32[]{:S(2)}, u32[]{:S(2)}) collective-permute-start(f32[4,26,1,128]{3,0,2,1:T(4,128)S(1)} %copy.195), channel_id=1, source_target_pairs={{1,0},{2,1},{3,2},{4,3},{5,4},{6,5},{7,6},{0,7},{9,8},{10,9},{11,1... | collective-permute-start | bytes 159752 | tf_op jit(solution)/shard_map/ppermute | solution.py:22
  179.5 5.2 %slice-start = ((s8[6291456]{0:T(1024)(128)(4,1)}), s8[4194304]{0:T(1024)(128)(4,1)S(1)}, s32[]{:S(2)}) async-start(s8[6291456]{0:T(1024)(128)(4,1)} %bitcast.101), calls=%async_computation | async-start | bytes 8388608
  179.5 5.2 %slice-start.4 = ((s8[4718592]{0:T(1024)(128)(4,1)}), s8[4194304]{0:T(1024)(128)(4,1)S(1)}, s32[]{:S(2)}) async-start(s8[4718592]{0:T(1024)(128)(4,1)} %bitcast.105), calls=%async_computation.4 | async-start | bytes 8388608
  179.5 6.4 %slice-start.8 = ((s8[4681728]{0:T(1024)(128)(4,1)}), s8[4194304]{0:T(1024)(128)(4,1)S(1)}, s32[]{:S(2)}) async-start(s8[4681728]{0:T(1024)(128)(4,1)} %bitcast.110), calls=%async_computation.8 | async-start | bytes 8388608
  180.4 6.3 %slice-start.1 = ((s8[6291456]{0:T(1024)(128)(4,1)}), s8[2097152]{0:T(1024)(128)(4,1)S(1)}, s32[]{:S(2)}) async-start(s8[6291456]{0:T(1024)(128)(4,1)} %bitcast.101), calls=%async_computation.1 | async-start | bytes 4194304
  180.4 6.3 %slice-start.5 = ((s8[4718592]{0:T(1024)(128)(4,1)}), s8[524288]{0:T(1024)(128)(4,1)S(1)}, s32[]{:S(2)}) async-start(s8[4718592]{0:T(1024)(128)(4,1)} %bitcast.105), calls=%async_computation.5 | async-start | bytes 1048576
  180.4 6.4 %slice-start.9 = ((s8[4681728]{0:T(1024)(128)(4,1)}), s8[487424]{0:T(1024)(128)(4,1)S(1)}, s32[]{:S(2)}) async-start(s8[4681728]{0:T(1024)(128)(4,1)} %bitcast.110), calls=%async_computation.9 | async-start | bytes 974848
  200.6 5.5 %copy-start.1 = (f32[3,24,32,128]{2,1,3,0:T(8,128)}, f32[3,24,32,128]{2,1,3,0:T(8,128)S(1)}, u32[]{:S(2)}) copy-start(f32[3,24,32,128]{2,1,3,0:T(8,128)S(1)} %fusion.19) | copy-start | bytes 3538948
  201.9 5.9 %copy-start.2 = (f32[24,32,128]{1,0,2:T(8,128)}, f32[24,32,128]{1,0,2:T(8,128)S(1)}, u32[]{:S(2)}) copy-start(f32[24,32,128]{1,0,2:T(8,128)S(1)} %slice_bitcast_fusion.1) | copy-start | bytes 1179652
  206.1 8.3 %collective-permute-start.9 = (f32[3,1,32,128]{2,1,3,0:T(1,128)}, f32[3,1,32,128]{2,1,3,0:T(1,128)S(1)}, u32[]{:S(2)}, u32[]{:S(2)}) collective-permute-start(f32[3,1,32,128]{2,1,3,0:T(1,128)} %get-tuple-element.28), channel_id=1, source_target_pairs={{0,8},{8,16},{16,24},{24,0},{1,9},{9,17},{17,25},{25,1},{2,10},{10... | collective-permute-start | bytes 147464 | tf_op jit(solution)/shard_map/ppermute | solution.py:20
  206.1 8.4 %collective-permute-start.8 = (f32[3,1,32,128]{2,1,3,0:T(1,128)S(1)}, f32[3,1,32,128]{2,1,3,0:T(1,128)S(1)}, u32[]{:S(2)}, u32[]{:S(2)}) collective-permute-start(f32[3,1,32,128]{2,1,3,0:T(1,128)S(1)} %get-tuple-element.29), channel_id=1, source_target_pairs={{8,0},{16,8},{24,16},{0,24},{9,1},{17,9},{25,17},{1,25},{10,2},{18... | collective-permute-start | bytes 147464 | tf_op jit(solution)/shard_map/ppermute | solution.py:22
  214.5 7.4 %copy-start.10 = (f32[3,1,32,128]{2,1,3,0:T(1,128)}, f32[3,1,32,128]{2,1,3,0:T(1,128)S(1)}, u32[]{:S(2)}) copy-start(f32[3,1,32,128]{2,1,3,0:T(1,128)S(1)} %collective-permute-done.8) | copy-start | bytes 147460
  214.7 7.2 %collective-permute-start.11 = (f32[3,26,1,128]{3,2,1,0:T(1,128)S(1)}, f32[3,26,1,128]{3,2,1,0:T(1,128)S(1)}, u32[]{:S(2)}, u32[]{:S(2)}) collective-permute-start(f32[3,26,1,128]{3,2,1,0:T(1,128)S(1)} %get-tuple-element.66), channel_id=1, source_target_pairs={{0,1},{1,2},{2,3},{3,4},{4,5},{5,6},{6,7},{7,0},{8,9},{9,10},{10,1... | collective-permute-start | bytes 119816 | tf_op jit(solution)/shard_map/ppermute | solution.py:20
  215.9 6.0 %collective-permute-start.10 = (f32[3,26,1,128]{3,2,1,0:T(1,128)S(1)}, f32[3,26,1,128]{3,2,1,0:T(1,128)S(1)}, u32[]{:S(2)}, u32[]{:S(2)}) collective-permute-start(f32[3,26,1,128]{3,2,1,0:T(1,128)S(1)} %get-tuple-element.67), channel_id=1, source_target_pairs={{1,0},{2,1},{3,2},{4,3},{5,4},{6,5},{7,6},{0,7},{9,8},{10,9},{11,1... | collective-permute-start | bytes 119816 | tf_op jit(solution)/shard_map/ppermute | solution.py:22
  235.8 3.7 %collective-permute-start.12 = (f32[4,1,32,128]{3,2,1,0:T(8,128)S(1)}, f32[4,1,32,128]{3,2,1,0:T(8,128)S(1)}, u32[]{:S(2)}, u32[]{:S(2)}) collective-permute-start(f32[4,1,32,128]{3,2,1,0:T(8,128)S(1)} %get-tuple-element.58), channel_id=1, source_target_pairs={{0,8},{8,16},{16,24},{24,0},{1,9},{9,17},{17,25},{25,1},{2,10},{10... | collective-permute-start | bytes 196616 | tf_op jit(solution)/shard_map/ppermute | solution.py:20
  235.9 3.7 %collective-permute-start.13 = (f32[4,1,32,128]{3,2,1,0:T(8,128)S(1)}, f32[4,1,32,128]{3,2,1,0:T(8,128)S(1)}, u32[]{:S(2)}, u32[]{:S(2)}) collective-permute-start(f32[4,1,32,128]{3,2,1,0:T(8,128)S(1)} %get-tuple-element.59), channel_id=1, source_target_pairs={{8,0},{16,8},{24,16},{0,24},{9,1},{17,9},{25,17},{1,25},{10,2},{18... | collective-permute-start | bytes 196616 | tf_op jit(solution)/shard_map/ppermute | solution.py:22
  239.7 1.2 copy-start.4
  241.6 28.1 %collective-permute-start.14 = (f32[4,26,1,128]{3,0,2,1:T(4,128)S(1)}, f32[4,26,1,128]{3,0,2,1:T(4,128)S(1)}, u32[]{:S(2)}, u32[]{:S(2)}) collective-permute-start(f32[4,26,1,128]{3,0,2,1:T(4,128)S(1)} %copy.232), channel_id=1, source_target_pairs={{0,1},{1,2},{2,3},{3,4},{4,5},{5,6},{6,7},{7,0},{8,9},{9,10},{10,1... | collective-permute-start | bytes 159752 | tf_op jit(solution)/shard_map/ppermute | solution.py:20
  241.7 23.1 %collective-permute-start.15 = (f32[4,26,1,128]{3,0,2,1:T(4,128)}, f32[4,26,1,128]{3,0,2,1:T(4,128)S(1)}, u32[]{:S(2)}, u32[]{:S(2)}) collective-permute-start(f32[4,26,1,128]{3,0,2,1:T(4,128)} %copy.233), channel_id=1, source_target_pairs={{1,0},{2,1},{3,2},{4,3},{5,4},{6,5},{7,6},{0,7},{9,8},{10,9},{11,1... | collective-permute-start | bytes 159752 | tf_op jit(solution)/shard_map/ppermute | solution.py:22
  257.0 4.5 %copy-start.5 = (f32[3,24,32,128]{3,2,1,0:T(8,128)S(1)}, f32[3,24,32,128]{3,2,1,0:T(8,128)}, u32[]{:S(2)}) copy-start(f32[3,24,32,128]{3,2,1,0:T(8,128)} %get-tuple-element.57) | copy-start | bytes 3538948
  278.6 5.3 %slice-start.2 = ((s8[4718592]{0:T(1024)(128)(4,1)}), s8[4194304]{0:T(1024)(128)(4,1)S(1)}, s32[]{:S(2)}) async-start(s8[4718592]{0:T(1024)(128)(4,1)} %bitcast.103), calls=%async_computation.2 | async-start | bytes 8388608
  278.6 5.3 %slice-start.6 = ((s8[4718592]{0:T(1024)(128)(4,1)}), s8[4194304]{0:T(1024)(128)(4,1)S(1)}, s32[]{:S(2)}) async-start(s8[4718592]{0:T(1024)(128)(4,1)} %bitcast.107), calls=%async_computation.6 | async-start | bytes 8388608
  279.5 4.4 %slice-start.3 = ((s8[4718592]{0:T(1024)(128)(4,1)}), s8[524288]{0:T(1024)(128)(4,1)S(1)}, s32[]{:S(2)}) async-start(s8[4718592]{0:T(1024)(128)(4,1)} %bitcast.103), calls=%async_computation.3 | async-start | bytes 1048576
  279.5 4.4 %slice-start.7 = ((s8[4718592]{0:T(1024)(128)(4,1)}), s8[524288]{0:T(1024)(128)(4,1)S(1)}, s32[]{:S(2)}) async-start(s8[4718592]{0:T(1024)(128)(4,1)} %bitcast.107), calls=%async_computation.7 | async-start | bytes 1048576
  282.4 1.5 copy-start.14
  308.8 7.1 %collective-permute-start.16 = (f32[3,1,32,128]{2,1,3,0:T(1,128)}, f32[3,1,32,128]{2,1,3,0:T(1,128)S(1)}, u32[]{:S(2)}, u32[]{:S(2)}) collective-permute-start(f32[3,1,32,128]{2,1,3,0:T(1,128)} %get-tuple-element.22), channel_id=1, source_target_pairs={{8,0},{16,8},{24,16},{0,24},{9,1},{17,9},{25,17},{1,25},{10,2},{18... | collective-permute-start | bytes 147464 | tf_op jit(solution)/shard_map/ppermute | solution.py:22
  310.3 7.2 %collective-permute-start.17 = (f32[3,1,32,128]{2,1,3,0:T(1,128)S(1)}, f32[3,1,32,128]{2,1,3,0:T(1,128)S(1)}, u32[]{:S(2)}, u32[]{:S(2)}) collective-permute-start(f32[3,1,32,128]{2,1,3,0:T(1,128)S(1)} %get-tuple-element.23), channel_id=1, source_target_pairs={{0,8},{8,16},{16,24},{24,0},{1,9},{9,17},{17,25},{25,1},{2,10},{10... | collective-permute-start | bytes 147464 | tf_op jit(solution)/shard_map/ppermute | solution.py:20
  315.8 9.3 %copy-start.3 = (f32[3,24,32,128]{3,2,1,0:T(8,128)}, f32[3,24,32,128]{3,2,1,0:T(8,128)S(1)}, u32[]{:S(2)}) copy-start(f32[3,24,32,128]{3,2,1,0:T(8,128)S(1)} %copy.225) | copy-start | bytes 3538948
  315.8 8.5 %copy-start.8 = (f32[3,1,32,128]{2,1,3,0:T(1,128)}, f32[3,1,32,128]{2,1,3,0:T(1,128)S(1)}, u32[]{:S(2)}) copy-start(f32[3,1,32,128]{2,1,3,0:T(1,128)S(1)} %collective-permute-done.16) | copy-start | bytes 147460
  315.9 8.4 %copy-start.11 = (f32[3,1,32,128]{3,2,1,0:T(8,128)}, f32[3,1,32,128]{3,2,1,0:T(8,128)S(1)}, u32[]{:S(2)}) copy-start(f32[3,1,32,128]{3,2,1,0:T(8,128)S(1)} %copy.222) | copy-start | bytes 147460
  317.4 6.9 %copy-start.9 = (f32[3,1,32,128]{2,1,3,0:T(1,128)}, f32[3,1,32,128]{2,1,3,0:T(1,128)S(1)}, u32[]{:S(2)}) copy-start(f32[3,1,32,128]{2,1,3,0:T(1,128)S(1)} %collective-permute-done.17) | copy-start | bytes 147460
  317.5 6.8 %copy-start.12 = (f32[3,1,32,128]{3,2,1,0:T(8,128)}, f32[3,1,32,128]{3,2,1,0:T(8,128)S(1)}, u32[]{:S(2)}) copy-start(f32[3,1,32,128]{3,2,1,0:T(8,128)S(1)} %copy.220) | copy-start | bytes 147460
  317.6 6.7 %collective-permute-start.19 = (f32[3,26,1,128]{3,2,1,0:T(1,128)S(1)}, f32[3,26,1,128]{3,2,1,0:T(1,128)S(1)}, u32[]{:S(2)}, u32[]{:S(2)}) collective-permute-start(f32[3,26,1,128]{3,2,1,0:T(1,128)S(1)} %get-tuple-element.62), channel_id=1, source_target_pairs={{0,1},{1,2},{2,3},{3,4},{4,5},{5,6},{6,7},{7,0},{8,9},{9,10},{10,1... | collective-permute-start | bytes 119816 | tf_op jit(solution)/shard_map/ppermute | solution.py:20
  317.7 6.7 %collective-permute-start.18 = (f32[3,26,1,128]{3,2,1,0:T(1,128)S(1)}, f32[3,26,1,128]{3,2,1,0:T(1,128)S(1)}, u32[]{:S(2)}, u32[]{:S(2)}) collective-permute-start(f32[3,26,1,128]{3,2,1,0:T(1,128)S(1)} %get-tuple-element.63), channel_id=1, source_target_pairs={{1,0},{2,1},{3,2},{4,3},{5,4},{6,5},{7,6},{0,7},{9,8},{10,9},{11,1... | collective-permute-start | bytes 119816 | tf_op jit(solution)/shard_map/ppermute | solution.py:22
where the time goes:
time: 341 us; the launch traced here: 335 us
  local copies, waits for them, and re-layouts  175 us (51%)
  other arithmetic  104 us (30%)
  starting transfers between devices  34.7 us (10%)
  waiting for transfers between devices  19.1 us (6%)
    reshape x2, local copies, waits for them, and re-layouts, block_mean(): field.reshape(leading + (sizes_a // 4, 4, sizes_b // 4, 4, sizes_c // 4, 4))  54.7 us
    add x3, other arithmetic, velocity_update(): return middle + relaxation * residual / diagonal  34.6 us
    ppermute x10, starting transfers between devices, with_halo(): lax.ppermute(head, axis, [((i + 1) % count, i) for i in range(count)])  30.8 us
    unnamed x61, local copies, waits for them, and re-layouts  27.9 us
    reduce_sum x2, other arithmetic, block_mean(): return shaped.mean(axis=(-5, -3, -1))  19.6 us
    slice x4, local copies, waits for them, and re-layouts, with_halo(): head = lax.slice_in_dim(cells, 0, width, axis=dim)  15.4 us
    ppermute x10, waiting for transfers between devices, with_halo(): lax.ppermute(tail, axis, [(i, (i + 1) % count) for i in range(count)])  14 us
    sub x2, other arithmetic, shards(): press_now = state_now[3] - pressure_step * divergence(rimmed_velocity, 1.0)  13.6 us
  transfers between devices with their start and end apart: 20, of which 11 were waited for; matrix products, arithmetic and copies ran while one was open for 15% of the time, Pallas kernels for 0%

commit v1 on v0

v1 whole, which is shorter than its diff:
```python
import functools

import jax
import jax.numpy as jnp
from jax import lax
from jax.experimental import pallas as pl
from jax.experimental.pallas import tpu as pltpu
from jax.sharding import PartitionSpec as P

viscosity = 1.0
penalty = 10.0
relaxation = 0.8
pressure_step = 1.0
mean_drive = 1.0

keep = 1.0 - relaxation
pore_step = relaxation / (6.0 * viscosity)
solid_step = relaxation / (6.0 * viscosity + penalty)

x_depths = ((0, 3), (1, 2), (2, 2), (3, 3))
y_depths = ((0, 2), (1, 3), (2, 2), (3, 3))
corner_cells = ((0, 1, 1), (0, 1, 2), (1, 1, 1), (1, 2, 1), (3, 1, 1), (3, 1, 2), (3, 2, 1))


def roll(value, shift):
    return pltpu.roll(value, shift % value.shape[-1], value.ndim - 1)


def lane_phase(shape):
    return lax.broadcasted_iota(jnp.int32, shape, len(shape) - 1) % 4


def step_of(mask):
    return jnp.where(mask != 0, solid_step, pore_step).astype(jnp.float32)


def pack_kernel(sizes, mask_ref, force_ref, mp_ref, mm_ref, xp_ref, xm_ref, yp_ref, ym_ref, sums):
    X, Y, Z = sizes
    cx, cy = X // 4, Y // 4

    def rows(field, index):
        if field == 3:
            return mask_ref[index, :]
        base = field * X * Y
        moved = pl.ds(base + index.start, index.size, index.stride)
        return force_ref[moved, :]

    def values(field, start, size, stride=1):
        taken = rows(field, pl.ds(start, size, stride))
        return step_of(taken) if field == 3 else taken

    phase = lane_phase((cy, Z))
    means = []
    for field in range(4):
        for block in range(cx):
            total = None
            for plane in range(4):
                part = rows(field, pl.ds((4 * block + plane) * Y, Y)).astype(jnp.float32)
                total = part if total is None else total + part
            sums[field, block] = total
    for block in range(cx):
        packed = None
        for field in range(4):
            total = sums[field, block, pl.ds(0, cy, 4), :]
            for row in range(1, 4):
                total = total + sums[field, block, pl.ds(row, cy, 4), :]
            total = total + jnp.where(phase % 2 == 0, roll(total, -1), roll(total, 1))
            total = total + jnp.where(phase < 2, roll(total, -2), roll(total, 2))
            mean = total * (1.0 / 64.0)
            if field == 0:
                mean = mean + mean_drive
            packed = mean if packed is None else jnp.where(phase == field, mean, packed)
        mp_ref[block] = packed
        mm_ref[block] = packed
    for ref, high in ((mp_ref, True), (mm_ref, False)):
        for top in (True, False):
            for number, (field, dx, dy) in enumerate(corner_cells):
                x = X - dx if high else dx - 1
                y = Y - dy if top else dy - 1
                ref[cx + (0 if top else 1), pl.ds(number, 1), :] = values(field, x * Y + y, 1)
            ref[cx + (0 if top else 1), pl.ds(7, 1), :] = jnp.zeros((1, Z), jnp.float32)
    for ref, high in ((xp_ref, True), (xm_ref, False)):
        number = 0
        for field, depth in x_depths:
            for plane in range(depth):
                x = X - depth + plane if high else plane
                ref[number] = values(field, x * Y, Y)
                number += 1
    for ref, high in ((yp_ref, True), (ym_ref, False)):
        number = 0
        for field, depth in y_depths:
            for row in range(depth):
                y = Y - depth + row if high else row
                ref[number] = values(field, y, X, Y)
                number += 1


def solve_kernel(sizes, *refs):
    X, Y, Z = sizes
    cx, cy = X // 4, Y // 4
    coarse_in = refs[:9]
    xl_ref, xr_ref, yd_ref, yu_ref, mask_ref, force_ref = refs[9:15]
    velo_out, press_out = refs[15:17]
    (cpk, corners, cforce, cstep, cvel, cvel2, cpress, cfine, yfine, force, step, mask, yd, yu, state, mid, sems) = refs[17:]
    ex, ey, fy = 4, 16, 8

    copies = []

    def copy(src, dst):
        made = pltpu.make_async_copy(src, dst, sems.at[len(copies)])
        made.start()
        copies.append(made)
        return made

    first = []
    for a in range(3):
        for b in range(3):
            first.append(copy(coarse_in[3 * a + b].at[pl.ds(0, cx)], cpk.at[pl.ds(a * cx, cx), pl.ds(b * cy, cy), :]))
    second = []
    for number, (a, b) in enumerate(((0, 0), (0, 2), (2, 0), (2, 2))):
        second.append(copy(coarse_in[3 * a + b].at[cx + (0 if b == 0 else 1)], corners.at[number]))
    second.append(copy(yd_ref, yd))
    second.append(copy(yu_ref, yu))
    second.append(copy(mask_ref, mask))
    for field in range(3):
        second.append(copy(force_ref.at[field], force.at[field, pl.ds(ex, X), pl.ds(fy, Y), :]))
    for ref, high in ((xl_ref, False), (xr_ref, True)):
        number = 0
        for field, depth in x_depths:
            x = ex + X if high else ex - depth
            target = step.at[pl.ds(x, depth), pl.ds(fy, Y), :] if field == 3 else force.at[field, pl.ds(x, depth), pl.ds(fy, Y), :]
            second.append(copy(ref.at[pl.ds(number, depth)], target))
            number += depth

    for made in first:
        made.wait()

    tall = 3 * cy
    mid_rows, up_rows, down_rows = pl.ds(cy, tall), pl.ds(cy + 1, tall), pl.ds(cy - 1, tall)
    phase = lane_phase((tall, Z))
    for x in range(3 * cx):
        packed = cpk[x]
        moved = {k: (packed if k == 0 else roll(packed, k)) for k in range(-3, 4)}
        spread = []
        for field in range(4):
            value = moved[3 - field]
            for t in range(3):
                value = jnp.where(phase == t, moved[t - field], value)
            spread.append(value)
        ratio = relaxation / (6.0 * viscosity / 16.0 + penalty * spread[3])
        cstep[x] = ratio
        for a in range(3):
            cforce[a, x] = spread[a]
            cvel[a, x, mid_rows, :] = ratio * spread[a]

    def coarse_div(vel, x):
        along_z = vel[2, x, mid_rows, :]
        total = (vel[0, x + 1, mid_rows, :] - vel[0, x - 1, mid_rows, :]) + (vel[1, x, up_rows, :] - vel[1, x, down_rows, :])
        return (total + (roll(along_z, -4) - roll(along_z, 4))) * 0.125

    for x in range(2, 3 * cx - 2):
        cpress[x, mid_rows, :] = -pressure_step * coarse_div(cvel, x)
    for x in range(3, 3 * cx - 3):
        ratio = cstep[x]
        press = cpress[x, mid_rows, :]
        slopes = (
            cpress[x + 1, mid_rows, :] - cpress[x - 1, mid_rows, :],
            cpress[x, up_rows, :] - cpress[x, down_rows, :],
            roll(press, -4) - roll(press, 4),
        )
        for a in range(3):
            middle = cvel[a, x, mid_rows, :]
            near = cvel[a, x + 1, mid_rows, :] + cvel[a, x - 1, mid_rows, :]
            near = near + (cvel[a, x, up_rows, :] + cvel[a, x, down_rows, :])
            near = near + (roll(middle, 4) + roll(middle, -4))
            source = cforce[a, x] - 0.125 * slopes[a] + (viscosity / 16.0) * near
            cvel2[a, x, mid_rows, :] = keep * middle + ratio * source
    weight = phase.astype(jnp.float32)
    weight = ((phase + 2) % 4).astype(jnp.float32) * 0.25 + 0.125

    def stretch_z(value):
        return (1.0 - weight) * roll(value, 2) + weight * roll(value, -2)

    for number in range(cx + 4):
        x = number + cx - 2
        press = cpress[x, mid_rows, :] - pressure_step * coarse_div(cvel2, x)
        cfine[3, number] = stretch_z(press)
        for a in range(3):
            cfine[a, number] = stretch_z(cvel2[a, x, mid_rows, :])
    count = cy + 4
    for field in range(4):
        for x in range(cx + 4):
            low = cfine[field, x, pl.ds(cy - 3, count), :]
            here = cfine[field, x, pl.ds(cy - 2, count), :]
            high = cfine[field, x, pl.ds(cy - 1, count), :]
            yfine[field, x, pl.ds(0, count, 4), :] = 0.375 * low + 0.625 * here
            yfine[field, x, pl.ds(1, count, 4), :] = 0.125 * low + 0.875 * here
            yfine[field, x, pl.ds(2, count, 4), :] = 0.875 * here + 0.125 * high
            yfine[field, x, pl.ds(3, count, 4), :] = 0.625 * here + 0.375 * high

    wide = Y + 16
    wide_rows = pl.ds(ey - 8, wide)

    def stretch_x(m, carry):
        for field in range(4):
            low, here, high = yfine[field, m], yfine[field, m + 1], yfine[field, m + 2]
            state[field, 4 * m, wide_rows, :] = 0.375 * low + 0.625 * here
            state[field, 4 * m + 1, wide_rows, :] = 0.125 * low + 0.875 * here
            state[field, 4 * m + 2, wide_rows, :] = 0.875 * here + 0.125 * high
            state[field, 4 * m + 3, wide_rows, :] = 0.625 * here + 0.375 * high
        return carry

    lax.fori_loop(0, cx + 2, stretch_x, 0)

    for made in second:
        made.wait()
    for x in range(X):
        step[ex + x, pl.ds(fy, Y), :] = step_of(mask[x])
    for ref, high in ((yd, False), (yu, True)):
        number = 0
        for field, depth in y_depths:
            for row in range(depth):
                y = fy + Y + row if high else fy - depth + row
                for x in range(X):
                    line = ref[number, pl.ds(x, 1), :]
                    if field == 3:
                        step[ex + x, pl.ds(y, 1), :] = line
                    else:
                        force[field, ex + x, pl.ds(y, 1), :] = line
                number += 1
    for number, (a, b) in enumerate(((0, 0), (0, 2), (2, 0), (2, 2))):
        for row, (field, dx, dy) in enumerate(corner_cells):
            x = ex - dx if a == 0 else ex + X - 1 + dx
            y = fy - dy if b == 0 else fy + Y - 1 + dy
            line = corners[number, pl.ds(row, 1), :]
            if field == 3:
                step[x, pl.ds(y, 1), :] = line
            else:
                force[field, x, pl.ds(y, 1), :] = line

    def move(old, new, x, components, start, size):
        rows, above, below = pl.ds(ey + start, size), pl.ds(ey + start + 1, size), pl.ds(ey + start - 1, size)
        source_rows = pl.ds(fy + start, size)
        ratio = step[x, source_rows, :]
        for a in components:
            if a == 0:
                slope = state[3, x + 1, rows, :] - state[3, x - 1, rows, :]
            elif a == 1:
                slope = state[3, x, above, :] - state[3, x, below, :]
            else:
                press = state[3, x, rows, :]
                slope = roll(press, -1) - roll(press, 1)
            middle = old[a, x, rows, :]
            near = old[a, x + 1, rows, :] + old[a, x - 1, rows, :]
            near = near + (old[a, x, above, :] + old[a, x, below, :])
            near = near + (roll(middle, 1) + roll(middle, -1))
            source = force[a, x, source_rows, :]
            if a == 0:
                source = source + mean_drive
            source = source - 0.5 * slope + near
            new[a, x, rows, :] = keep * middle + ratio * source

    def divergence(vel, x, start, size):
        rows, above, below = pl.ds(ey + start, size), pl.ds(ey + start + 1, size), pl.ds(ey + start - 1, size)
        along_z = vel[2, x, rows, :]
        total = (vel[0, x + 1, rows, :] - vel[0, x - 1, rows, :]) + (vel[1, x, above, :] - vel[1, x, below, :])
        return (total + (roll(along_z, -1) - roll(along_z, 1))) * (0.5 * pressure_step)

    def loop(low, high, body):
        def run(x, carry):
            body(x)
            return carry

        lax.fori_loop(low, high, run, 0)

    loop(1, X + 7, lambda x: move(state, mid, x, (0, 1, 2), -8, wide))

    def press_first(x):
        state[3, x, wide_rows, :] = state[3, x, wide_rows, :] - divergence(mid, x, -8, wide)

    loop(2, X + 6, press_first)
    move(mid, state, ex - 1, (0,), 0, Y)
    move(mid, state, ex + X, (0,), 0, Y)

    def second_move(x):
        move(mid, state, x, (0, 2), 0, Y)
        move(mid, state, x, (1,), -8, wide)

    loop(ex, ex + X, second_move)
    inner = pl.ds(ey, Y)
    last = [copy(state.at[a, pl.ds(ex, X), inner, :], velo_out.at[a]) for a in range(3)]

    def press_second(x):
        mask_rows = state[3, x, inner, :] - divergence(state, x, 0, Y)
        step[x, pl.ds(fy, Y), :] = mask_rows

    loop(ex, ex + X, press_second)
    last.append(copy(step.at[pl.ds(ex, X), pl.ds(fy, Y), :], press_out))
    for made in last:
        made.wait()


def shift(value, axis, by):
    count = lax.axis_size(axis)
    return lax.ppermute(value, axis, [(i, (i + by) % count) for i in range(count)])


def shards(solid_mask, forcing):
    X, Y, Z = sizes = solid_mask.shape
    cx, cy = X // 4, Y // 4
    f32 = jnp.float32
    made = jax.ShapeDtypeStruct
    message = made((cx + 2, 8, Z), f32)
    planes = made((10, Y, Z), f32)
    lines = made((10, X, Z), f32)
    mp, mm, xp, xm, yp, ym = pl.pallas_call(
        functools.partial(pack_kernel, sizes),
        out_shape=(message, message, planes, planes, lines, lines),
        scratch_shapes=[pltpu.VMEM((4, cx, Y, Z), f32)],
        compiler_params=pltpu.CompilerParams(vmem_limit_bytes=40 * 2**20),
        name="pack",
    )(solid_mask.reshape(X * Y, Z), forcing.reshape(3 * X * Y, Z))
    ml = shift(mp, "grp", 1)
    mr = shift(mm, "grp", -1)
    xl = shift(xp, "grp", 1)
    xr = shift(xm, "grp", -1)
    own = (ml, mp, mr)
    up = [shift(value, "dev", -1) for value in own]
    down = [shift(value, "dev", 1) for value in own]
    yu = shift(ym, "dev", -1)
    yd = shift(yp, "dev", 1)
    blocks = []
    for a in range(3):
        blocks += [down[a], own[a], up[a]]
    anywhere = pl.BlockSpec(memory_space=pl.ANY)
    tall = 3 * cy
    vmem = pltpu.VMEM
    return pl.pallas_call(
        functools.partial(solve_kernel, sizes),
        out_shape=(made((3, X, Y, Z), f32), made((X, Y, Z), f32)),
        in_specs=[anywhere] * 15,
        out_specs=(anywhere, anywhere),
        scratch_shapes=[
            vmem((3 * cx, tall, Z), f32),
            vmem((4, 8, Z), f32),
            vmem((3, 3 * cx, tall, Z), f32),
            vmem((3 * cx, tall, Z), f32),
            vmem((3, 3 * cx, tall + 2 * cy, Z), f32),
            vmem((3, 3 * cx, tall + 2 * cy, Z), f32),
            vmem((3 * cx, tall + 2 * cy, Z), f32),
            vmem((4, cx + 4, tall, Z), f32),
            vmem((4, cx + 4, Y + 16, Z), f32),
            vmem((3, X + 8, Y + 16, Z), f32),
            vmem((X + 8, Y + 16, Z), f32),
            vmem((X, Y, Z), jnp.int32),
            vmem((10, X, Z), f32),
            vmem((10, X, Z), f32),
            vmem((4, X + 8, Y + 32, Z), f32),
            vmem((3, X + 8, Y + 32, Z), f32),
            pltpu.SemaphoreType.DMA((40,)),
        ],
        compiler_params=pltpu.CompilerParams(vmem_limit_bytes=56 * 2**20),
        name="solve",
    )(*blocks, xl, xr, yd, yu, solid_mask, forcing)


def solution(mesh):
    in_specs = (P("grp", "dev", None), P(None, "grp", "dev", None))
    out_specs = (P(None, "grp", "dev", None), P("grp", "dev", None))
    return jax.shard_map(shards, mesh=mesh, in_specs=in_specs, out_specs=out_specs, check_vma=False)
```

time: 341 us -> 57.4 us (0.17); the launches traced: 335 us -> 57.2 us
  local copies, waits for them, and re-layouts: 175 us -> 3.63 us
  other arithmetic: 104 us -> 0 us
  starting transfers between devices: 34.7 us -> 18.3 us
  Pallas kernels: 0 us -> 15.4 us
    reshape x2 -> x0, local copies, waits for them, and re-layouts: 54.7 us -> none  [block_mean(): field.reshape(leading + (sizes_a // 4, 4, sizes_b // 4, 4, sizes_c // 4, 4))]
    add x9 -> x0, other arithmetic: 47.4 us -> none  [the longest x3 34.6 us: velocity_update(): return middle + relaxation * residual / diagonal]
    slice x24 -> x0, local copies, waits for them, and re-layouts: 40.3 us -> none  [the longest x4 15.4 us: with_halo(): head = lax.slice_in_dim(cells, 0, width, axis=dim)]
    unnamed x61 -> x30, local copies, waits for them, and re-layouts: 27.9 us -> 3.63 us
    ppermute x8 -> x0, local copies, waits for them, and re-layouts: 19.8 us -> none  [the longest x4 9.93 us: with_halo(): lax.ppermute(tail, axis, [(i, (i + 1) % count) for i in range(count)])]
    reduce_sum x2 -> x0, other arithmetic: 19.6 us -> none  [block_mean(): return shaped.mean(axis=(-5, -3, -1))]
    sub x6 -> x0, other arithmetic: 16.7 us -> none  [the longest x2 13.6 us: shards(): press_now = state_now[3] - pressure_step * divergence(rimmed_velocity, 1.0)]
    ppermute x20 -> x12, starting transfers between devices: 34.7 us -> 18.3 us  [shift(): lax.ppermute(value, axis, [(i, (i + by) % count) for i in range(count)])]
  transfers between devices with their start and end apart: 20 -> 12, of which waited for: 11 -> 4; matrix products, arithmetic and copies ran while one was open for 15% -> 0% of each run, Pallas kernels for 0% -> 0%
where the time goes in v1:
time: 57.4 us; the launch traced here: 57.2 us
  waiting for transfers between devices  19 us (33%)
  starting transfers between devices  18.3 us (32%)
  Pallas kernels  15.4 us (27%)
  local copies, waits for them, and re-layouts  3.63 us (6%)
  between operations  0.81 us (1%)
    ppermute x12, waiting for transfers between devices, shift(): lax.ppermute(value, axis, [(i, (i + by) % count) for i in range(count)])  19 us
    ppermute x12, starting transfers between devices, shift(): lax.ppermute(value, axis, [(i, (i + by) % count) for i in range(count)])  18.3 us
    pallas_call x1, Pallas kernels, shards(): pl.pallas_call(functools.partial(solve_kernel, sizes), out_shape=(made((3...  15.1 us
    unnamed x30, local copies, waits for them, and re-layouts  3.63 us
  transfers between devices with their start and end apart: 12, of which 4 were waited for; matrix products, arithmetic and copies ran while one was open for 0% of the time, Pallas kernels for 0%

profile of v1, /device:TPU:0, one launch (start us, length us, event | category | flops | bytes accessed | tf_op | source)
XLA Modules:
  0.0 57.2 jit_solution(4332855919773045311)
XLA Ops:
  0.6 0.0 copy-start
  0.6 1.3 %copy-done = f32[3,24,32,128]{3,2,1,0:T(8,128)S(1)} copy-done((f32[3,24,32,128]{3,2,1,0:T(8,128)S(1)}, f32[3,24,32,128]{3,2,1,0:T(8,128)}, u32[]{:S(2)}) %copy-start) | copy-done | bytes 1179672
  1.9 0.0 copy-start.1
  1.9 1.0 %copy-done.1 = s32[24,32,128]{2,1,0:T(8,128)S(1)} copy-done((s32[24,32,128]{2,1,0:T(8,128)S(1)}, s32[24,32,128]{2,1,0:T(8,128)}, u32[]{:S(2)}) %copy-start.1) | copy-done | bytes 393240
  2.9 0.3 pack.1
  3.2 0.0 copy-start.2
  3.3 2.4 %collective-permute-start.5 = (f32[8,8,128]{2,1,0:T(8,128)S(1)}, f32[8,8,128]{2,1,0:T(8,128)S(1)}, u32[]{:S(2)}, u32[]{:S(2)}) collective-permute-start(f32[8,8,128]{2,1,0:T(8,128)S(1)} %get-tuple-element.9), channel_id=1, source_target_pairs={{0,24},{8,0},{16,8},{24,16},{1,25},{9,1},{17,9},{25,17},{2,26},{10... | collective-permute-start | bytes 98312 | tf_op jit(solution)/shard_map/ppermute | solution.py:305
  5.7 4.6 %collective-permute-start.4 = (f32[8,8,128]{2,1,0:T(8,128)S(1)}, f32[8,8,128]{2,1,0:T(8,128)S(1)}, u32[]{:S(2)}, u32[]{:S(2)}) collective-permute-start(f32[8,8,128]{2,1,0:T(8,128)S(1)} %get-tuple-element.8.refs_4_), channel_id=1, source_target_pairs={{0,7},{1,0},{2,1},{3,2},{4,3},{5,4},{6,5},{7,6},{8,15},{9,8},{10,9... | collective-permute-start | bytes 98312 | tf_op jit(solution)/shard_map/ppermute | solution.py:305
  10.2 0.0 collective-permute-start.8
  10.2 1.7 %collective-permute-start.9 = (f32[10,32,128]{2,1,0:T(8,128)S(1)}, f32[10,32,128]{2,1,0:T(8,128)S(1)}, u32[]{:S(2)}, u32[]{:S(2)}) collective-permute-start(f32[10,32,128]{2,1,0:T(8,128)S(1)} %get-tuple-element.11), channel_id=1, source_target_pairs={{0,24},{8,0},{16,8},{24,16},{1,25},{9,1},{17,9},{25,17},{2,26},{10... | collective-permute-start | bytes 491528 | tf_op jit(solution)/shard_map/ppermute | solution.py:305
  12.0 0.0 collective-permute-start.3
  12.0 0.0 collective-permute-done.5.refs_7_
  12.0 0.0 copy-start.7
  12.0 0.1 collective-permute-start
  12.1 0.0 collective-permute-done.4.refs_5_
  12.1 0.0 copy-start.8
  12.1 4.8 %collective-permute-start.7 = (f32[8,8,128]{2,1,0:T(8,128)S(1)}, f32[8,8,128]{2,1,0:T(8,128)S(1)}, u32[]{:S(2)}, u32[]{:S(2)}) collective-permute-start(f32[8,8,128]{2,1,0:T(8,128)S(1)} %collective-permute-done.5.refs_7_), channel_id=1, source_target_pairs={{0,7},{1,0},{2,1},{3,2},{4,3},{5,4},{6,5},{7,6},{8,15},{9,8},{10,9... | collective-permute-start | bytes 98312 | tf_op jit(solution)/shard_map/ppermute | solution.py:305
  16.9 1.7 %collective-permute-done.3.refs_3_ = f32[8,8,128]{2,1,0:T(8,128)S(1)} collective-permute-done((f32[8,8,128]{2,1,0:T(8,128)S(1)}, f32[8,8,128]{2,1,0:T(8,128)S(1)}, u32[]{:S(2)}, u32[]{:S(2)}) %collective-permute-start.3) | collective-permute-done | bytes 32800 | tf_op jit(solution)/shard_map/ppermute | solution.py:305
  18.6 0.0 copy-start.9
  18.6 0.0 collective-permute-start.10
  18.6 0.0 collective-permute-done.refs_1_
  18.6 0.0 copy-start.10
  18.6 4.7 %collective-permute-start.11 = (f32[10,24,128]{2,1,0:T(8,128)S(1)}, f32[10,24,128]{2,1,0:T(8,128)S(1)}, u32[]{:S(2)}, u32[]{:S(2)}) collective-permute-start(f32[10,24,128]{2,1,0:T(8,128)S(1)} %get-tuple-element.13), channel_id=1, source_target_pairs={{0,7},{1,0},{2,1},{3,2},{4,3},{5,4},{6,5},{7,6},{8,15},{9,8},{10,9... | collective-permute-start | bytes 368648 | tf_op jit(solution)/shard_map/ppermute | solution.py:305
  23.3 0.0 collective-permute-done.7.refs_8_
  23.3 0.0 copy-start.11
  23.3 0.0 collective-permute-start.6
  23.3 6.7 %collective-permute-done.6.refs_6_ = f32[8,8,128]{2,1,0:T(8,128)S(1)} collective-permute-done((f32[8,8,128]{2,1,0:T(8,128)S(1)}, f32[8,8,128]{2,1,0:T(8,128)S(1)}, u32[]{:S(2)}, u32[]{:S(2)}) %collective-permute-start.6) | collective-permute-done | bytes 32800 | tf_op jit(solution)/shard_map/ppermute | solution.py:305
  30.1 0.0 copy-start.12
  30.1 0.0 collective-permute-start.2
  30.1 3.9 %collective-permute-done.2.refs_2_ = f32[8,8,128]{2,1,0:T(8,128)S(1)} collective-permute-done((f32[8,8,128]{2,1,0:T(8,128)S(1)}, f32[8,8,128]{2,1,0:T(8,128)S(1)}, u32[]{:S(2)}, u32[]{:S(2)}) %collective-permute-start.2) | collective-permute-done | bytes 32800 | tf_op jit(solution)/shard_map/ppermute | solution.py:305
  34.0 0.0 copy-start.13
  34.0 0.0 collective-permute-start.1
  34.0 6.6 %collective-permute-done.1.refs_0_ = f32[8,8,128]{2,1,0:T(8,128)S(1)} collective-permute-done((f32[8,8,128]{2,1,0:T(8,128)S(1)}, f32[8,8,128]{2,1,0:T(8,128)S(1)}, u32[]{:S(2)}, u32[]{:S(2)}) %collective-permute-start.1) | collective-permute-done | bytes 32800 | tf_op jit(solution)/shard_map/ppermute | solution.py:305
  40.6 0.0 copy-start.14
  40.6 0.0 collective-permute-done.10.refs_11_
  40.6 0.0 copy-start.5
  40.6 0.0 collective-permute-done.11.refs_12_
  40.6 0.0 copy-start.6
  40.6 0.0 collective-permute-done.8.refs_9_
  40.6 0.0 copy-start.3
  40.6 0.0 collective-permute-done.9.refs_10_
  40.6 0.0 copy-done.2
  40.7 0.0 copy-done.7
  40.7 0.0 copy-done.8
  40.7 0.0 copy-done.9
  40.7 0.0 copy-done.10
  40.7 0.0 copy-done.11
  40.7 0.0 copy-done.12
  40.7 0.0 copy-done.13
  40.7 0.5 copy-done.14
  41.2 0.1 copy-done.5
  41.3 0.1 copy-done.6
  41.3 0.1 copy-done.3
  41.4 0.0 copy-start.4
  41.4 0.7 %copy-done.4 = f32[10,32,128]{2,1,0:T(8,128)} copy-done((f32[10,32,128]{2,1,0:T(8,128)}, f32[10,32,128]{2,1,0:T(8,128)S(1)}, u32[]{:S(2)}) %copy-start.4) | copy-done | bytes 163864
  42.1 15.1 %solve.1 = (f32[3,24,32,128]{3,2,1,0:T(8,128)}, f32[24,32,128]{2,1,0:T(8,128)}) custom-call(f32[8,8,128]{2,1,0:T(8,128)} %copy-done.14, f32[8,8,128]{2,1,0:T(8,128)} %copy-done.10, f32[8,8,128]{2,1,0:T(8,128)} %copy-done.13, f32[8,8,128]{2,1,0:T(8,128)} %copy-done.9, f32[8,8,128]{2,1,0:T(8,128)} %copy-done.2, f32[8,8,128]{2,1,0:T(8,128)} %copy-done.8, ...), custom_call_target="tpu_custom_call" | custom-call | tf_op jit(solution)/shard_map/solve/pallas_call | solution.py:338
Async XLA Ops:
  0.6 1.3 %copy-start = (f32[3,24,32,128]{3,2,1,0:T(8,128)S(1)}, f32[3,24,32,128]{3,2,1,0:T(8,128)}, u32[]{:S(2)}) copy-start(f32[3,24,32,128]{3,2,1,0:T(8,128)} %refs_14_.1) | copy-start | bytes 3538948
  1.9 1.0 %copy-start.1 = (s32[24,32,128]{2,1,0:T(8,128)S(1)}, s32[24,32,128]{2,1,0:T(8,128)}, u32[]{:S(2)}) copy-start(s32[24,32,128]{2,1,0:T(8,128)} %refs_13_.1) | copy-start | bytes 1179652
  3.2 37.4 %copy-start.2 = (f32[8,8,128]{2,1,0:T(8,128)}, f32[8,8,128]{2,1,0:T(8,128)S(1)}, u32[]{:S(2)}) copy-start(f32[8,8,128]{2,1,0:T(8,128)S(1)} %get-tuple-element.8.refs_4_) | copy-start | bytes 98308
  3.3 8.7 %collective-permute-start.5 = (f32[8,8,128]{2,1,0:T(8,128)S(1)}, f32[8,8,128]{2,1,0:T(8,128)S(1)}, u32[]{:S(2)}, u32[]{:S(2)}) collective-permute-start(f32[8,8,128]{2,1,0:T(8,128)S(1)} %get-tuple-element.9), channel_id=1, source_target_pairs={{0,24},{8,0},{16,8},{24,16},{1,25},{9,1},{17,9},{25,17},{2,26},{10... | collective-permute-start | bytes 98312 | tf_op jit(solution)/shard_map/ppermute | solution.py:305
  5.7 6.4 %collective-permute-start.4 = (f32[8,8,128]{2,1,0:T(8,128)S(1)}, f32[8,8,128]{2,1,0:T(8,128)S(1)}, u32[]{:S(2)}, u32[]{:S(2)}) collective-permute-start(f32[8,8,128]{2,1,0:T(8,128)S(1)} %get-tuple-element.8.refs_4_), channel_id=1, source_target_pairs={{0,7},{1,0},{2,1},{3,2},{4,3},{5,4},{6,5},{7,6},{8,15},{9,8},{10,9... | collective-permute-start | bytes 98312 | tf_op jit(solution)/shard_map/ppermute | solution.py:305
  10.2 30.4 %collective-permute-start.8 = (f32[10,32,128]{2,1,0:T(8,128)S(1)}, f32[10,32,128]{2,1,0:T(8,128)S(1)}, u32[]{:S(2)}, u32[]{:S(2)}) collective-permute-start(f32[10,32,128]{2,1,0:T(8,128)S(1)} %get-tuple-element.10), channel_id=1, source_target_pairs={{0,8},{8,16},{16,24},{24,0},{1,9},{9,17},{17,25},{25,1},{2,10},{10... | collective-permute-start | bytes 491528 | tf_op jit(solution)/shard_map/ppermute | solution.py:305
  10.2 30.4 %collective-permute-start.9 = (f32[10,32,128]{2,1,0:T(8,128)S(1)}, f32[10,32,128]{2,1,0:T(8,128)S(1)}, u32[]{:S(2)}, u32[]{:S(2)}) collective-permute-start(f32[10,32,128]{2,1,0:T(8,128)S(1)} %get-tuple-element.11), channel_id=1, source_target_pairs={{0,24},{8,0},{16,8},{24,16},{1,25},{9,1},{17,9},{25,17},{2,26},{10... | collective-permute-start | bytes 491528 | tf_op jit(solution)/shard_map/ppermute | solution.py:305
  12.0 6.6 %collective-permute-start.3 = (f32[8,8,128]{2,1,0:T(8,128)S(1)}, f32[8,8,128]{2,1,0:T(8,128)S(1)}, u32[]{:S(2)}, u32[]{:S(2)}) collective-permute-start(f32[8,8,128]{2,1,0:T(8,128)S(1)} %get-tuple-element.8.refs_4_), channel_id=1, source_target_pairs={{0,1},{1,2},{2,3},{3,4},{4,5},{5,6},{6,7},{7,0},{8,9},{9,10},{10,1... | collective-permute-start | bytes 98312 | tf_op jit(solution)/shard_map/ppermute | solution.py:305
  12.0 28.7 %copy-start.7 = (f32[8,8,128]{2,1,0:T(8,128)}, f32[8,8,128]{2,1,0:T(8,128)S(1)}, u32[]{:S(2)}) copy-start(f32[8,8,128]{2,1,0:T(8,128)S(1)} %collective-permute-done.5.refs_7_) | copy-start | bytes 98308
  12.0 6.6 %collective-permute-start = (f32[8,8,128]{2,1,0:T(8,128)S(1)}, f32[8,8,128]{2,1,0:T(8,128)S(1)}, u32[]{:S(2)}, u32[]{:S(2)}) collective-permute-start(f32[8,8,128]{2,1,0:T(8,128)S(1)} %get-tuple-element.8.refs_4_), channel_id=1, source_target_pairs={{0,8},{8,16},{16,24},{24,0},{1,9},{9,17},{17,25},{25,1},{2,10},{10... | collective-permute-start | bytes 98312 | tf_op jit(solution)/shard_map/ppermute | solution.py:305
  12.1 28.6 %copy-start.8 = (f32[8,8,128]{2,1,0:T(8,128)}, f32[8,8,128]{2,1,0:T(8,128)S(1)}, u32[]{:S(2)}) copy-start(f32[8,8,128]{2,1,0:T(8,128)S(1)} %collective-permute-done.4.refs_5_) | copy-start | bytes 98308
  12.1 11.2 %collective-permute-start.7 = (f32[8,8,128]{2,1,0:T(8,128)S(1)}, f32[8,8,128]{2,1,0:T(8,128)S(1)}, u32[]{:S(2)}, u32[]{:S(2)}) collective-permute-start(f32[8,8,128]{2,1,0:T(8,128)S(1)} %collective-permute-done.5.refs_7_), channel_id=1, source_target_pairs={{0,7},{1,0},{2,1},{3,2},{4,3},{5,4},{6,5},{7,6},{8,15},{9,8},{10,9... | collective-permute-start | bytes 98312 | tf_op jit(solution)/shard_map/ppermute | solution.py:305
  18.6 22.1 %copy-start.9 = (f32[8,8,128]{2,1,0:T(8,128)}, f32[8,8,128]{2,1,0:T(8,128)S(1)}, u32[]{:S(2)}) copy-start(f32[8,8,128]{2,1,0:T(8,128)S(1)} %collective-permute-done.3.refs_3_) | copy-start | bytes 98308
  18.6 22.0 %collective-permute-start.10 = (f32[10,24,128]{2,1,0:T(8,128)S(1)}, f32[10,24,128]{2,1,0:T(8,128)S(1)}, u32[]{:S(2)}, u32[]{:S(2)}) collective-permute-start(f32[10,24,128]{2,1,0:T(8,128)S(1)} %get-tuple-element.12), channel_id=1, source_target_pairs={{0,1},{1,2},{2,3},{3,4},{4,5},{5,6},{6,7},{7,0},{8,9},{9,10},{10,1... | collective-permute-start | bytes 368648 | tf_op jit(solution)/shard_map/ppermute | solution.py:305
  18.6 22.1 %copy-start.10 = (f32[8,8,128]{2,1,0:T(8,128)}, f32[8,8,128]{2,1,0:T(8,128)S(1)}, u32[]{:S(2)}) copy-start(f32[8,8,128]{2,1,0:T(8,128)S(1)} %collective-permute-done.refs_1_) | copy-start | bytes 98308
  18.6 22.0 %collective-permute-start.11 = (f32[10,24,128]{2,1,0:T(8,128)S(1)}, f32[10,24,128]{2,1,0:T(8,128)S(1)}, u32[]{:S(2)}, u32[]{:S(2)}) collective-permute-start(f32[10,24,128]{2,1,0:T(8,128)S(1)} %get-tuple-element.13), channel_id=1, source_target_pairs={{0,7},{1,0},{2,1},{3,2},{4,3},{5,4},{6,5},{7,6},{8,15},{9,8},{10,9... | collective-permute-start | bytes 368648 | tf_op jit(solution)/shard_map/ppermute | solution.py:305
  23.3 17.4 %copy-start.11 = (f32[8,8,128]{2,1,0:T(8,128)}, f32[8,8,128]{2,1,0:T(8,128)S(1)}, u32[]{:S(2)}) copy-start(f32[8,8,128]{2,1,0:T(8,128)S(1)} %collective-permute-done.7.refs_8_) | copy-start | bytes 98308
  23.3 6.7 %collective-permute-start.6 = (f32[8,8,128]{2,1,0:T(8,128)S(1)}, f32[8,8,128]{2,1,0:T(8,128)S(1)}, u32[]{:S(2)}, u32[]{:S(2)}) collective-permute-start(f32[8,8,128]{2,1,0:T(8,128)S(1)} %collective-permute-done.5.refs_7_), channel_id=1, source_target_pairs={{0,1},{1,2},{2,3},{3,4},{4,5},{5,6},{6,7},{7,0},{8,9},{9,10},{10,1... | collective-permute-start | bytes 98312 | tf_op jit(solution)/shard_map/ppermute | solution.py:305
  30.1 10.6 %copy-start.12 = (f32[8,8,128]{2,1,0:T(8,128)}, f32[8,8,128]{2,1,0:T(8,128)S(1)}, u32[]{:S(2)}) copy-start(f32[8,8,128]{2,1,0:T(8,128)S(1)} %collective-permute-done.6.refs_6_) | copy-start | bytes 98308
  30.1 3.9 %collective-permute-start.2 = (f32[8,8,128]{2,1,0:T(8,128)S(1)}, f32[8,8,128]{2,1,0:T(8,128)S(1)}, u32[]{:S(2)}, u32[]{:S(2)}) collective-permute-start(f32[8,8,128]{2,1,0:T(8,128)S(1)} %collective-permute-done.refs_1_), channel_id=1, source_target_pairs={{0,7},{1,0},{2,1},{3,2},{4,3},{5,4},{6,5},{7,6},{8,15},{9,8},{10,9... | collective-permute-start | bytes 98312 | tf_op jit(solution)/shard_map/ppermute | solution.py:305
  34.0 6.7 %copy-start.13 = (f32[8,8,128]{2,1,0:T(8,128)}, f32[8,8,128]{2,1,0:T(8,128)S(1)}, u32[]{:S(2)}) copy-start(f32[8,8,128]{2,1,0:T(8,128)S(1)} %collective-permute-done.2.refs_2_) | copy-start | bytes 98308
  34.0 6.6 %collective-permute-start.1 = (f32[8,8,128]{2,1,0:T(8,128)S(1)}, f32[8,8,128]{2,1,0:T(8,128)S(1)}, u32[]{:S(2)}, u32[]{:S(2)}) collective-permute-start(f32[8,8,128]{2,1,0:T(8,128)S(1)} %collective-permute-done.refs_1_), channel_id=1, source_target_pairs={{0,1},{1,2},{2,3},{3,4},{4,5},{5,6},{6,7},{7,0},{8,9},{9,10},{10,1... | collective-permute-start | bytes 98312 | tf_op jit(solution)/shard_map/ppermute | solution.py:305
  40.6 0.6 %copy-start.14 = (f32[8,8,128]{2,1,0:T(8,128)}, f32[8,8,128]{2,1,0:T(8,128)S(1)}, u32[]{:S(2)}) copy-start(f32[8,8,128]{2,1,0:T(8,128)S(1)} %collective-permute-done.1.refs_0_) | copy-start | bytes 98308
  40.6 0.7 %copy-start.5 = (f32[10,24,128]{2,1,0:T(8,128)}, f32[10,24,128]{2,1,0:T(8,128)S(1)}, u32[]{:S(2)}) copy-start(f32[10,24,128]{2,1,0:T(8,128)S(1)} %collective-permute-done.10.refs_11_) | copy-start | bytes 368644
  40.6 0.7 %copy-start.6 = (f32[10,24,128]{2,1,0:T(8,128)}, f32[10,24,128]{2,1,0:T(8,128)S(1)}, u32[]{:S(2)}) copy-start(f32[10,24,128]{2,1,0:T(8,128)S(1)} %collective-permute-done.11.refs_12_) | copy-start | bytes 368644
  40.6 0.8 %copy-start.3 = (f32[10,32,128]{2,1,0:T(8,128)}, f32[10,32,128]{2,1,0:T(8,128)S(1)}, u32[]{:S(2)}) copy-start(f32[10,32,128]{2,1,0:T(8,128)S(1)} %collective-permute-done.8.refs_9_) | copy-start | bytes 491524
  41.4 0.7 %copy-start.4 = (f32[10,32,128]{2,1,0:T(8,128)}, f32[10,32,128]{2,1,0:T(8,128)S(1)}, u32[]{:S(2)}) copy-start(f32[10,32,128]{2,1,0:T(8,128)S(1)} %collective-permute-done.9.refs_10_) | copy-start | bytes 491524

commit v2 on v1

--- a/solution.py
+++ b/solution.py
@@ -34,9 +34,19 @@
     return jnp.where(mask != 0, solid_step, pore_step).astype(jnp.float32)
 
 
-def pack_kernel(sizes, mask_ref, force_ref, mp_ref, mm_ref, xp_ref, xm_ref, yp_ref, ym_ref, sums):
+def pack_kernel(sizes, mask_in, force_in, mp_ref, mm_ref, xp_ref, xm_ref, yp_ref, ym_ref, mask_ref, force_ref, sums, sems):
     X, Y, Z = sizes
     cx, cy = X // 4, Y // 4
+    copies = [
+        pltpu.make_async_copy(mask_in, mask_ref, sems.at[3]),
+    ]
+    for field in range(3):
+        part = pl.ds(field * X * Y, X * Y)
+        copies.append(pltpu.make_async_copy(force_in.at[part], force_ref.at[part], sems.at[field]))
+    for made in copies:
+        made.start()
+    for made in copies:
+        made.wait()
 
     def rows(field, index):
         if field == 3:
@@ -91,17 +101,18 @@
         for field, depth in y_depths:
             for row in range(depth):
                 y = Y - depth + row if high else row
-                ref[number] = values(field, y, X, Y)
+                line = values(field, y, X, Y)
+                for tile in range(X // 8):
+                    ref[number * (X // 8) + tile] = line[8 * tile : 8 * tile + 8]
                 number += 1
 
 
 def solve_kernel(sizes, *refs):
     X, Y, Z = sizes
     cx, cy = X // 4, Y // 4
-    coarse_in = refs[:9]
-    xl_ref, xr_ref, yd_ref, yu_ref, mask_ref, force_ref = refs[9:15]
-    velo_out, press_out = refs[15:17]
-    (cpk, corners, cforce, cstep, cvel, cvel2, cpress, cfine, yfine, force, step, mask, yd, yu, state, mid, sems) = refs[17:]
+    down_ref, up_ref, ml_ref, mp_ref, mr_ref, xl_ref, xr_ref, mask, force_ref = refs[:9]
+    velo_out, press_out = refs[9:11]
+    (cforce, cstep, cvel, cvel2, cpress, cfine, yfine, force, step, state, mid, sems) = refs[11:]
     ex, ey, fy = 4, 16, 8
 
     copies = []
@@ -112,16 +123,7 @@
         copies.append(made)
         return made
 
-    first = []
-    for a in range(3):
-        for b in range(3):
-            first.append(copy(coarse_in[3 * a + b].at[pl.ds(0, cx)], cpk.at[pl.ds(a * cx, cx), pl.ds(b * cy, cy), :]))
     second = []
-    for number, (a, b) in enumerate(((0, 0), (0, 2), (2, 0), (2, 2))):
-        second.append(copy(coarse_in[3 * a + b].at[cx + (0 if b == 0 else 1)], corners.at[number]))
-    second.append(copy(yd_ref, yd))
-    second.append(copy(yu_ref, yu))
-    second.append(copy(mask_ref, mask))
     for field in range(3):
         second.append(copy(force_ref.at[field], force.at[field, pl.ds(ex, X), pl.ds(fy, Y), :]))
     for ref, high in ((xl_ref, False), (xr_ref, True)):
@@ -132,14 +134,12 @@
             second.append(copy(ref.at[pl.ds(number, depth)], target))
             number += depth
 
-    for made in first:
-        made.wait()
-
     tall = 3 * cy
     mid_rows, up_rows, down_rows = pl.ds(cy, tall), pl.ds(cy + 1, tall), pl.ds(cy - 1, tall)
     phase = lane_phase((tall, Z))
     for x in range(3 * cx):
-        packed = cpk[x]
+        middle_ref = (ml_ref, mp_ref, mr_ref)[x // cx]
+        packed = jnp.concatenate([down_ref[x], middle_ref[x % cx], up_ref[x]], 0)
         moved = {k: (packed if k == 0 else roll(packed, k)) for k in range(-3, 4)}
         spread = []
         for field in range(4):
@@ -216,27 +216,28 @@
         made.wait()
     for x in range(X):
         step[ex + x, pl.ds(fy, Y), :] = step_of(mask[x])
-    for ref, high in ((yd, False), (yu, True)):
+    for ref, high in ((down_ref, False), (up_ref, True)):
         number = 0
         for field, depth in y_depths:
             for row in range(depth):
                 y = fy + Y + row if high else fy - depth + row
                 for x in range(X):
-                    line = ref[number, pl.ds(x, 1), :]
+                    place = number * X + x
+                    line = ref[3 * cx + 2 + place // 8, pl.ds(place % 8, 1), :]
                     if field == 3:
                         step[ex + x, pl.ds(y, 1), :] = line
                     else:
                         force[field, ex + x, pl.ds(y, 1), :] = line
                 number += 1
-    for number, (a, b) in enumerate(((0, 0), (0, 2), (2, 0), (2, 2))):
-        for row, (field, dx, dy) in enumerate(corner_cells):
-            x = ex - dx if a == 0 else ex + X - 1 + dx
-            y = fy - dy if b == 0 else fy + Y - 1 + dy
-            line = corners[number, pl.ds(row, 1), :]
-            if field == 3:
-                step[x, pl.ds(y, 1), :] = line
-            else:
-                force[field, x, pl.ds(y, 1), :] = line
+        for side in range(2):
+            for row, (field, dx, dy) in enumerate(corner_cells):
+                x = ex - dx if side == 0 else ex + X - 1 + dx
+                y = fy + Y - 1 + dy if high else fy - dy
+                line = ref[3 * cx + side, pl.ds(row, 1), :]
+                if field == 3:
+                    step[x, pl.ds(y, 1), :] = line
+                else:
+                    force[field, x, pl.ds(y, 1), :] = line
 
     def move(old, new, x, components, start, size):
         rows, above, below = pl.ds(ey + start, size), pl.ds(ey + start + 1, size), pl.ds(ey + start - 1, size)
@@ -271,7 +272,7 @@
             body(x)
             return carry
 
-        lax.fori_loop(low, high, run, 0)
+        lax.fori_loop(low, high, run, 0, unroll=10)
 
     loop(1, X + 7, lambda x: move(state, mid, x, (0, 1, 2), -8, wide))
 
@@ -298,6 +299,17 @@
     last.append(copy(step.at[pl.ds(ex, X), pl.ds(fy, Y), :], press_out))
     for made in last:
         made.wait()
+
+
+def relay_kernel(sizes, ml_ref, mp_ref, mr_ref, yp_ref, ym_ref, up_ref, down_ref):
+    X, Y, Z = sizes
+    cx = X // 4
+    for ref, lines, corner in ((down_ref, yp_ref, cx), (up_ref, ym_ref, cx + 1)):
+        for number, source in enumerate((ml_ref, mp_ref, mr_ref)):
+            ref[pl.ds(number * cx, cx)] = source[pl.ds(0, cx)]
+        ref[3 * cx] = ml_ref[corner]
+        ref[3 * cx + 1] = mr_ref[corner]
+        ref[pl.ds(3 * cx + 2, 10 * X // 8)] = lines[...]
 
 
 def shift(value, axis, by):
@@ -310,39 +322,46 @@
     cx, cy = X // 4, Y // 4
     f32 = jnp.float32
     made = jax.ShapeDtypeStruct
+    vmem = pltpu.VMEM
+    anywhere = pl.BlockSpec(memory_space=pl.ANY)
+    near = pl.BlockSpec(memory_space=vmem)
     message = made((cx + 2, 8, Z), f32)
     planes = made((10, Y, Z), f32)
-    lines = made((10, X, Z), f32)
-    mp, mm, xp, xm, yp, ym = pl.pallas_call(
+    lines = made((10 * X // 8, 8, Z), f32)
+    mp, mm, xp, xm, yp, ym, mask, force = pl.pallas_call(
         functools.partial(pack_kernel, sizes),
-        out_shape=(message, message, planes, planes, lines, lines),
-        scratch_shapes=[pltpu.VMEM((4, cx, Y, Z), f32)],
-        compiler_params=pltpu.CompilerParams(vmem_limit_bytes=40 * 2**20),
+        out_shape=(message, message, planes, planes, lines, lines, made((X * Y, Z), jnp.int32), made((3 * X * Y, Z), f32)),
+        in_specs=[pl.BlockSpec(memory_space=pltpu.HBM)] * 2,
+        out_specs=[near] * 8,
+        scratch_shapes=[vmem((4, cx, Y, Z), f32), pltpu.SemaphoreType.DMA((4,))],
+        compiler_params=pltpu.CompilerParams(vmem_limit_bytes=12 * 2**20),
         name="pack",
-    )(solid_mask.reshape(X * Y, Z), forcing.reshape(3 * X * Y, Z))
+    )(
+        pltpu.with_memory_space_constraint(solid_mask.reshape(X * Y, Z), pltpu.HBM),
+        pltpu.with_memory_space_constraint(forcing.reshape(3 * X * Y, Z), pltpu.HBM),
+    )
+    xl = shift(xp, "grp", 1)
+    xr = shift(xm, "grp", -1)
     ml = shift(mp, "grp", 1)
     mr = shift(mm, "grp", -1)
-    xl = shift(xp, "grp", 1)
-    xr = shift(xm, "grp", -1)
-    own = (ml, mp, mr)
-    up = [shift(value, "dev", -1) for value in own]
-    down = [shift(value, "dev", 1) for value in own]
-    yu = shift(ym, "dev", -1)
-    yd = shift(yp, "dev", 1)
-    blocks = []
-    for a in range(3):
-        blocks += [down[a], own[a], up[a]]
-    anywhere = pl.BlockSpec(memory_space=pl.ANY)
+    joined = made((3 * cx + 2 + 10 * X // 8, 8, Z), f32)
+    to_up, to_down = pl.pallas_call(
+        functools.partial(relay_kernel, sizes),
+        out_shape=(joined, joined),
+        in_specs=[near] * 5,
+        out_specs=[near] * 2,
+        compiler_params=pltpu.CompilerParams(vmem_limit_bytes=2 * 2**20),
+        name="relay",
+    )(ml, mp, mr, yp, ym)
+    up = shift(to_up, "dev", -1)
+    down = shift(to_down, "dev", 1)
     tall = 3 * cy
-    vmem = pltpu.VMEM
     return pl.pallas_call(
         functools.partial(solve_kernel, sizes),
         out_shape=(made((3, X, Y, Z), f32), made((X, Y, Z), f32)),
-        in_specs=[anywhere] * 15,
+        in_specs=[near] * 9,
         out_specs=(anywhere, anywhere),
         scratch_shapes=[
-            vmem((3 * cx, tall, Z), f32),
-            vmem((4, 8, Z), f32),
             vmem((3, 3 * cx, tall, Z), f32),
             vmem((3 * cx, tall, Z), f32),
             vmem((3, 3 * cx, tall + 2 * cy, Z), f32),
@@ -352,16 +371,13 @@
             vmem((4, cx + 4, Y + 16, Z), f32),
             vmem((3, X + 8, Y + 16, Z), f32),
             vmem((X + 8, Y + 16, Z), f32),
-            vmem((X, Y, Z), jnp.int32),
-            vmem((10, X, Z), f32),
-            vmem((10, X, Z), f32),
             vmem((4, X + 8, Y + 32, Z), f32),
             vmem((3, X + 8, Y + 32, Z), f32),
-            pltpu.SemaphoreType.DMA((40,)),
+            pltpu.SemaphoreType.DMA((20,)),
         ],
-        compiler_params=pltpu.CompilerParams(vmem_limit_bytes=56 * 2**20),
+        compiler_params=pltpu.CompilerParams(vmem_limit_bytes=32 * 2**20),
         name="solve",
-    )(*blocks, xl, xr, yd, yu, solid_mask, forcing)
+    )(down, up, ml, mp, mr, xl, xr, mask.reshape(X, Y, Z), force.reshape(3, X, Y, Z))
 
 
 def solution(mesh):

time: 57.4 us -> 28.5 us (0.50)
  waiting for transfers between devices: 19 us -> 8.41 us
  starting transfers between devices: 18.3 us -> 8.95 us
  Pallas kernels: 15.4 us -> 10.4 us
  local copies, waits for them, and re-layouts: 3.63 us -> 0 us
    ppermute x12 -> x6, waiting for transfers between devices: 19 us -> 8.41 us  [shift(): lax.ppermute(value, axis, [(i, (i + by) % count) for i in range(count)])]
    ppermute x12 -> x6, starting transfers between devices: 18.3 us -> 8.95 us  [shift(): lax.ppermute(value, axis, [(i, (i + by) % count) for i in range(count)])]
    pallas_call x1, Pallas kernels: 15.1 us -> 8.51 us  [shards(): pl.pallas_call(functools.partial(solve_kernel, sizes), out_shape=(made((3...]
    unnamed x30 -> x0, local copies, waits for them, and re-layouts: 3.63 us -> none
    pallas_call x1, Pallas kernels: 0.34 us -> 1.83 us  [shards(): pl.pallas_call(functools.partial(pack_kernel, sizes), out_shape=(message,...]
  transfers between devices with their start and end apart: 12 -> 6, of which waited for: 4 -> 4; matrix products, arithmetic and copies ran while one was open for 0% -> 0% of each run, Pallas kernels for 0% -> 0%
where the time goes in v2:
time: 28.5 us; the launch traced here: 28.4 us
  Pallas kernels  10.4 us (36%)
  starting transfers between devices  8.95 us (31%)
  waiting for transfers between devices  8.41 us (30%)
  between operations  0.65 us (2%)
    ppermute x6, starting transfers between devices, shift(): lax.ppermute(value, axis, [(i, (i + by) % count) for i in range(count)])  8.95 us
    pallas_call x1, Pallas kernels, shards(): pl.pallas_call(functools.partial(solve_kernel, sizes), out_shape=(made((3...  8.51 us
    ppermute x6, waiting for transfers between devices, shift(): lax.ppermute(value, axis, [(i, (i + by) % count) for i in range(count)])  8.41 us
    pallas_call x1, Pallas kernels, shards(): pl.pallas_call(functools.partial(pack_kernel, sizes), out_shape=(message,...  1.83 us
  transfers between devices with their start and end apart: 6, of which 4 were waited for; matrix products, arithmetic and copies ran while one was open for 0% of the time, Pallas kernels for 0%

profile of v2, /device:TPU:0, one launch (start us, length us, event | category | flops | bytes accessed | tf_op | source)
XLA Modules:
  0.0 28.4 jit_solution(8750084746765129930)
XLA Ops:
  0.6 1.8 %pack.1 = (f32[8,8,128]{2,1,0:T(8,128)S(1)}, f32[8,8,128]{2,1,0:T(8,128)S(1)}, f32[10,32,128]{2,1,0:T(8,128)S(1)}, f32[10,32,128]{2,1,0:T(8,128)S(1)}, f32[30,8,...) custom-call(s32[768,128]{1,0:T(8,128)} %bitcast.7, ...), custom_call_target="tpu_custom_call" | custom-call | tf_op jit(solution)/shard_map/pack/pallas_call | solution.py:331
  2.5 2.4 %collective-permute-start.1 = (f32[8,8,128]{2,1,0:T(8,128)S(1)}, f32[8,8,128]{2,1,0:T(8,128)S(1)}, u32[]{:S(2)}, u32[]{:S(2)}) collective-permute-start(f32[8,8,128]{2,1,0:T(8,128)S(1)} %get-tuple-element.13), channel_id=1, source_target_pairs={{0,24},{8,0},{16,8},{24,16},{1,25},{9,1},{17,9},{25,17},{2,26},{10... | collective-permute-start | bytes 98312 | tf_op jit(solution)/shard_map/ppermute | solution.py:317
  4.9 0.0 collective-permute-start
  4.9 1.7 %collective-permute-done.1.mr_ref.refs_4_ = f32[8,8,128]{2,1,0:T(8,128)S(1)} collective-permute-done((f32[8,8,128]{2,1,0:T(8,128)S(1)}, f32[8,8,128]{2,1,0:T(8,128)S(1)}, u32[]{:S(2)}, u32[]{:S(2)}) %collective-permute-start.1) | collective-permute-done | bytes 32800 | tf_op jit(solution)/shard_map/ppermute | solution.py:317
  6.6 1.6 %collective-permute-done.ml_ref.refs_2_ = f32[8,8,128]{2,1,0:T(8,128)S(1)} collective-permute-done((f32[8,8,128]{2,1,0:T(8,128)S(1)}, f32[8,8,128]{2,1,0:T(8,128)S(1)}, u32[]{:S(2)}, u32[]{:S(2)}) %collective-permute-start) | collective-permute-done | bytes 32800 | tf_op jit(solution)/shard_map/ppermute | solution.py:317
  8.3 1.6 %collective-permute-start.2 = (f32[50,8,128]{2,1,0:T(8,128)S(1)}, f32[50,8,128]{2,1,0:T(8,128)S(1)}, u32[]{:S(2)}, u32[]{:S(2)}) collective-permute-start(f32[50,8,128]{2,1,0:T(8,128)S(1)} %get-tuple-element.16), channel_id=1, source_target_pairs={{0,1},{1,2},{2,3},{3,4},{4,5},{5,6},{6,7},{7,0},{8,9},{9,10},{10,1... | collective-permute-start | bytes 614408 | tf_op jit(solution)/shard_map/ppermute | solution.py:317
  9.8 3.2 %collective-permute-start.3 = (f32[50,8,128]{2,1,0:T(8,128)S(1)}, f32[50,8,128]{2,1,0:T(8,128)S(1)}, u32[]{:S(2)}, u32[]{:S(2)}) collective-permute-start(f32[50,8,128]{2,1,0:T(8,128)S(1)} %get-tuple-element.17), channel_id=1, source_target_pairs={{0,7},{1,0},{2,1},{3,2},{4,3},{5,4},{6,5},{7,6},{8,15},{9,8},{10,9... | collective-permute-start | bytes 614408 | tf_op jit(solution)/shard_map/ppermute | solution.py:317
  13.0 0.0 collective-permute-start.4
  13.0 1.7 %collective-permute-start.5 = (f32[10,32,128]{2,1,0:T(8,128)S(1)}, f32[10,32,128]{2,1,0:T(8,128)S(1)}, u32[]{:S(2)}, u32[]{:S(2)}) collective-permute-start(f32[10,32,128]{2,1,0:T(8,128)S(1)} %get-tuple-element.19), channel_id=1, source_target_pairs={{0,24},{8,0},{16,8},{24,16},{1,25},{9,1},{17,9},{25,17},{2,26},{10... | collective-permute-start | bytes 491528 | tf_op jit(solution)/shard_map/ppermute | solution.py:317
  14.8 3.5 %collective-permute-done.4.refs_5_ = f32[10,32,128]{2,1,0:T(8,128)S(1)} collective-permute-done((f32[10,32,128]{2,1,0:T(8,128)S(1)}, f32[10,32,128]{2,1,0:T(8,128)S(1)}, u32[]{:S(2)}, u32[]{:S(2)}) %collective-permute-start.4) | collective-permute-done | bytes 163872 | tf_op jit(solution)/shard_map/ppermute | solution.py:317
  18.3 0.0 collective-permute-done.5.refs_6_
  18.3 0.0 collective-permute-done.2.refs_0_
  18.3 1.6 %collective-permute-done.3.refs_1_ = f32[50,8,128]{2,1,0:T(8,128)S(1)} collective-permute-done((f32[50,8,128]{2,1,0:T(8,128)S(1)}, f32[50,8,128]{2,1,0:T(8,128)S(1)}, u32[]{:S(2)}, u32[]{:S(2)}) %collective-permute-start.3) | collective-permute-done | bytes 204832 | tf_op jit(solution)/shard_map/ppermute | solution.py:317
  19.9 8.5 %solve.1 = (f32[3,24,32,128]{3,2,1,0:T(8,128)}, f32[24,32,128]{2,1,0:T(8,128)}) custom-call(f32[50,8,128]{2,1,0:T(8,128)S(1)} %collective-permute-done.2.refs_0_, f32[50,8,128]{2,1,0:T(8,128)S(1)} %collective-permute-done.3.refs_1_, f32[8,8,128]{2,1,0:T(8,128)S(1)} %collective-permute-done.ml_ref.refs_2_, f32[8,8,128]{2,1,0:T(8,128)S(1)} %get-tuple-element.12.mp_ref.refs_3_, ...), custom_call_target="tpu_custom_call" | custom-call | tf_op jit(solution)/shard_map/solve/pallas_call | solution.py:359
  (1 shorter events, 0.0 us)
Async XLA Ops:
  2.5 4.2 %collective-permute-start.1 = (f32[8,8,128]{2,1,0:T(8,128)S(1)}, f32[8,8,128]{2,1,0:T(8,128)S(1)}, u32[]{:S(2)}, u32[]{:S(2)}) collective-permute-start(f32[8,8,128]{2,1,0:T(8,128)S(1)} %get-tuple-element.13), channel_id=1, source_target_pairs={{0,24},{8,0},{16,8},{24,16},{1,25},{9,1},{17,9},{25,17},{2,26},{10... | collective-permute-start | bytes 98312 | tf_op jit(solution)/shard_map/ppermute | solution.py:317
  4.9 3.3 %collective-permute-start = (f32[8,8,128]{2,1,0:T(8,128)S(1)}, f32[8,8,128]{2,1,0:T(8,128)S(1)}, u32[]{:S(2)}, u32[]{:S(2)}) collective-permute-start(f32[8,8,128]{2,1,0:T(8,128)S(1)} %get-tuple-element.12.mp_ref.refs_3_), channel_id=1, source_target_pairs={{0,8},{8,16},{16,24},{24,0},{1,9},{9,17},{17,25},{25,1},{2,10},{10... | collective-permute-start | bytes 98312 | tf_op jit(solution)/shard_map/ppermute | solution.py:317
  8.3 10.0 %collective-permute-start.2 = (f32[50,8,128]{2,1,0:T(8,128)S(1)}, f32[50,8,128]{2,1,0:T(8,128)S(1)}, u32[]{:S(2)}, u32[]{:S(2)}) collective-permute-start(f32[50,8,128]{2,1,0:T(8,128)S(1)} %get-tuple-element.16), channel_id=1, source_target_pairs={{0,1},{1,2},{2,3},{3,4},{4,5},{5,6},{6,7},{7,0},{8,9},{9,10},{10,1... | collective-permute-start | bytes 614408 | tf_op jit(solution)/shard_map/ppermute | solution.py:317
  9.8 10.0 %collective-permute-start.3 = (f32[50,8,128]{2,1,0:T(8,128)S(1)}, f32[50,8,128]{2,1,0:T(8,128)S(1)}, u32[]{:S(2)}, u32[]{:S(2)}) collective-permute-start(f32[50,8,128]{2,1,0:T(8,128)S(1)} %get-tuple-element.17), channel_id=1, source_target_pairs={{0,7},{1,0},{2,1},{3,2},{4,3},{5,4},{6,5},{7,6},{8,15},{9,8},{10,9... | collective-permute-start | bytes 614408 | tf_op jit(solution)/shard_map/ppermute | solution.py:317
  13.0 5.2 %collective-permute-start.4 = (f32[10,32,128]{2,1,0:T(8,128)S(1)}, f32[10,32,128]{2,1,0:T(8,128)S(1)}, u32[]{:S(2)}, u32[]{:S(2)}) collective-permute-start(f32[10,32,128]{2,1,0:T(8,128)S(1)} %get-tuple-element.18), channel_id=1, source_target_pairs={{0,8},{8,16},{16,24},{24,0},{1,9},{9,17},{17,25},{25,1},{2,10},{10... | collective-permute-start | bytes 491528 | tf_op jit(solution)/shard_map/ppermute | solution.py:317
  13.0 5.2 %collective-permute-start.5 = (f32[10,32,128]{2,1,0:T(8,128)S(1)}, f32[10,32,128]{2,1,0:T(8,128)S(1)}, u32[]{:S(2)}, u32[]{:S(2)}) collective-permute-start(f32[10,32,128]{2,1,0:T(8,128)S(1)} %get-tuple-element.19), channel_id=1, source_target_pairs={{0,24},{8,0},{16,8},{24,16},{1,25},{9,1},{17,9},{25,17},{2,26},{10... | collective-permute-start | bytes 491528 | tf_op jit(solution)/shard_map/ppermute | solution.py:317

commit v3 on v2

--- a/solution.py
+++ b/solution.py
@@ -28,6 +28,24 @@
 
 def lane_phase(shape):
     return lax.broadcasted_iota(jnp.int32, shape, len(shape) - 1) % 4
+
+
+def neighbour_matrices(Z, distance):
+    source = lax.broadcasted_iota(jnp.int32, (2 * Z, Z), 0) % Z
+    target = lax.broadcasted_iota(jnp.int32, (2 * Z, Z), 1)
+    after = (source == (target + distance) % Z).astype(jnp.float32)
+    before = (source == (target + Z - distance) % Z).astype(jnp.float32)
+    return (after + before).astype(jnp.bfloat16), (after - before).astype(jnp.bfloat16)
+
+
+def apply(matrix, values):
+    high = values.astype(jnp.bfloat16)
+    low = (values - high.astype(jnp.float32)).astype(jnp.bfloat16)
+    return jnp.dot(jnp.concatenate([high, low], -1), matrix, preferred_element_type=jnp.float32)
+
+
+def flat(values):
+    return values.reshape(-1, values.shape[-1])
 
 
 def step_of(mask):
@@ -107,13 +125,85 @@
                 number += 1
 
 
+def coarse_kernel(sizes, down_ref, up_ref, ml_ref, mp_ref, mr_ref, yfine, cforce, cstep, cvel, cpress, cfine):
+    X, Y, Z = sizes
+    cx, cy = X // 4, Y // 4
+    tall, deep = 3 * cy, cx + 10
+    mid_rows, up_rows, down_rows = pl.ds(cy, tall), pl.ds(cy + 1, tall), pl.ds(cy - 1, tall)
+    source = lax.broadcasted_iota(jnp.int32, (2 * Z, 4 * Z), 0) % Z
+    target = lax.broadcasted_iota(jnp.int32, (2 * Z, 4 * Z), 1)
+    spread = (source == (target % Z) // 4 * 4 + target // Z).astype(jnp.float32).astype(jnp.bfloat16)
+    pair_sum, pair_gap = neighbour_matrices(Z, 4)
+    source = lax.broadcasted_iota(jnp.int32, (2 * Z, Z), 0) % Z
+    target = lax.broadcasted_iota(jnp.int32, (2 * Z, Z), 1)
+    part = ((target + 2) % 4).astype(jnp.float32) * 0.25 + 0.125
+    stretch = jnp.where(source == (target + Z - 2) % Z, 1.0 - part, 0.0) + jnp.where(source == (target + 2) % Z, part, 0.0)
+    stretch = stretch.astype(jnp.bfloat16)
+
+    packed = []
+    for x in range(deep):
+        number, plane = divmod(x + cx - 5, cx)
+        packed += [down_ref[x], (ml_ref, mp_ref, mr_ref)[number][plane], up_ref[x]]
+    fields = apply(spread, jnp.concatenate(packed, 0))
+    shape = (deep, tall, Z)
+    ratio = relaxation / (6.0 * viscosity / 16.0 + penalty * fields[:, 3 * Z :].reshape(shape))
+    cstep[...] = ratio
+    for a in range(3):
+        force = fields[:, a * Z : (a + 1) * Z].reshape(shape)
+        cforce[a] = force
+        cvel[0, a, :, mid_rows, :] = ratio * force
+
+    def coarse_div(number, low, count):
+        planes, right, left = pl.ds(low, count), pl.ds(low + 1, count), pl.ds(low - 1, count)
+        total = cvel[number, 0, right, mid_rows, :] - cvel[number, 0, left, mid_rows, :]
+        total = total + (cvel[number, 1, planes, up_rows, :] - cvel[number, 1, planes, down_rows, :])
+        along_z = apply(pair_gap, flat(cvel[number, 2, planes, mid_rows, :])).reshape(total.shape)
+        return (total + along_z) * (0.125 * pressure_step)
+
+    cpress[pl.ds(1, deep - 2), mid_rows, :] = -coarse_div(0, 1, deep - 2)
+    count = deep - 4
+    planes, right, left = pl.ds(2, count), pl.ds(3, count), pl.ds(1, count)
+    shape = (count, tall, Z)
+    slopes = (
+        cpress[right, mid_rows, :] - cpress[left, mid_rows, :],
+        cpress[planes, up_rows, :] - cpress[planes, down_rows, :],
+        apply(pair_gap, flat(cpress[planes, mid_rows, :])).reshape(shape),
+    )
+    for a in range(3):
+        middle = cvel[0, a, planes, mid_rows, :]
+        near = cvel[0, a, right, mid_rows, :] + cvel[0, a, left, mid_rows, :]
+        near = near + (cvel[0, a, planes, up_rows, :] + cvel[0, a, planes, down_rows, :])
+        near = near + apply(pair_sum, flat(middle)).reshape(shape)
+        moved = cforce[a, planes] - 0.125 * slopes[a] + (viscosity / 16.0) * near
+        cvel[1, a, planes, mid_rows, :] = keep * middle + cstep[planes] * moved
+    count = deep - 6
+    planes = pl.ds(3, count)
+    press = cpress[planes, mid_rows, :] - coarse_div(1, 3, count)
+    ends = [cvel[1, a, planes, mid_rows, :] for a in range(3)] + [press]
+    for field in range(4):
+        cfine[field] = apply(stretch, flat(ends[field])).reshape(count, tall, Z)
+    row = lax.broadcasted_iota(jnp.int32, (8, Z), 0)
+    lower = row < 2
+    upper = row >= 6
+    part = ((row + 2) % 4).astype(jnp.float32) * 0.25 + 0.125
+    for field in range(4):
+        for x in range(count):
+            for tile in range((Y + 16) // 8):
+                first = cy - 3 + 2 * tile
+                lines = [jnp.broadcast_to(cfine[field, x, pl.ds(first + k, 1), :], (8, Z)) for k in range(4)]
+                near = jnp.where(lower, lines[0], jnp.where(upper, lines[2], lines[1]))
+                far = jnp.where(lower, lines[1], jnp.where(upper, lines[3], lines[2]))
+                yfine[field, x, pl.ds(8 * tile, 8), :] = near + part * (far - near)
+
+
 def solve_kernel(sizes, *refs):
     X, Y, Z = sizes
-    cx, cy = X // 4, Y // 4
-    down_ref, up_ref, ml_ref, mp_ref, mr_ref, xl_ref, xr_ref, mask, force_ref = refs[:9]
-    velo_out, press_out = refs[9:11]
-    (cforce, cstep, cvel, cvel2, cpress, cfine, yfine, force, step, state, mid, sems) = refs[11:]
+    cx = X // 4
+    yfine, down_ref, up_ref, xl_ref, xr_ref, mask, force_ref = refs[:7]
+    velo_out, press_out = refs[7:9]
+    force, step, state, mid, sems = refs[9:]
     ex, ey, fy = 4, 16, 8
+    deep = cx + 10
 
     copies = []
 
@@ -133,70 +223,6 @@
             target = step.at[pl.ds(x, depth), pl.ds(fy, Y), :] if field == 3 else force.at[field, pl.ds(x, depth), pl.ds(fy, Y), :]
             second.append(copy(ref.at[pl.ds(number, depth)], target))
             number += depth
-
-    tall = 3 * cy
-    mid_rows, up_rows, down_rows = pl.ds(cy, tall), pl.ds(cy + 1, tall), pl.ds(cy - 1, tall)
-    phase = lane_phase((tall, Z))
-    for x in range(3 * cx):
-        middle_ref = (ml_ref, mp_ref, mr_ref)[x // cx]
-        packed = jnp.concatenate([down_ref[x], middle_ref[x % cx], up_ref[x]], 0)
-        moved = {k: (packed if k == 0 else roll(packed, k)) for k in range(-3, 4)}
-        spread = []
-        for field in range(4):
-            value = moved[3 - field]
-            for t in range(3):
-                value = jnp.where(phase == t, moved[t - field], value)
-            spread.append(value)
-        ratio = relaxation / (6.0 * viscosity / 16.0 + penalty * spread[3])
-        cstep[x] = ratio
-        for a in range(3):
-            cforce[a, x] = spread[a]
-            cvel[a, x, mid_rows, :] = ratio * spread[a]
-
-    def coarse_div(vel, x):
-        along_z = vel[2, x, mid_rows, :]
-        total = (vel[0, x + 1, mid_rows, :] - vel[0, x - 1, mid_rows, :]) + (vel[1, x, up_rows, :] - vel[1, x, down_rows, :])
-        return (total + (roll(along_z, -4) - roll(along_z, 4))) * 0.125
-
-    for x in range(2, 3 * cx - 2):
-        cpress[x, mid_rows, :] = -pressure_step * coarse_div(cvel, x)
-    for x in range(3, 3 * cx - 3):
-        ratio = cstep[x]
-        press = cpress[x, mid_rows, :]
-        slopes = (
-            cpress[x + 1, mid_rows, :] - cpress[x - 1, mid_rows, :],
-            cpress[x, up_rows, :] - cpress[x, down_rows, :],
-            roll(press, -4) - roll(press, 4),
-        )
-        for a in range(3):
-            middle = cvel[a, x, mid_rows, :]
-            near = cvel[a, x + 1, mid_rows, :] + cvel[a, x - 1, mid_rows, :]
-            near = near + (cvel[a, x, up_rows, :] + cvel[a, x, down_rows, :])
-            near = near + (roll(middle, 4) + roll(middle, -4))
-            source = cforce[a, x] - 0.125 * slopes[a] + (viscosity / 16.0) * near
-            cvel2[a, x, mid_rows, :] = keep * middle + ratio * source
-    weight = phase.astype(jnp.float32)
-    weight = ((phase + 2) % 4).astype(jnp.float32) * 0.25 + 0.125
-
-    def stretch_z(value):
-        return (1.0 - weight) * roll(value, 2) + weight * roll(value, -2)
-
-    for number in range(cx + 4):
-        x = number + cx - 2
-        press = cpress[x, mid_rows, :] - pressure_step * coarse_div(cvel2, x)
-        cfine[3, number] = stretch_z(press)
-        for a in range(3):
-            cfine[a, number] = stretch_z(cvel2[a, x, mid_rows, :])
-    count = cy + 4
-    for field in range(4):
-        for x in range(cx + 4):
-            low = cfine[field, x, pl.ds(cy - 3, count), :]
-            here = cfine[field, x, pl.ds(cy - 2, count), :]
-            high = cfine[field, x, pl.ds(cy - 1, count), :]
-            yfine[field, x, pl.ds(0, count, 4), :] = 0.375 * low + 0.625 * here
-            yfine[field, x, pl.ds(1, count, 4), :] = 0.125 * low + 0.875 * here
-            yfine[field, x, pl.ds(2, count, 4), :] = 0.875 * here + 0.125 * high
-            yfine[field, x, pl.ds(3, count, 4), :] = 0.625 * here + 0.375 * high
 
     wide = Y + 16
     wide_rows = pl.ds(ey - 8, wide)
@@ -223,7 +249,7 @@
                 y = fy + Y + row if high else fy - depth + row
                 for x in range(X):
                     place = number * X + x
-                    line = ref[3 * cx + 2 + place // 8, pl.ds(place % 8, 1), :]
+                    line = ref[deep + 2 + place // 8, pl.ds(place % 8, 1), :]
                     if field == 3:
                         step[ex + x, pl.ds(y, 1), :] = line
                     else:
@@ -233,83 +259,98 @@
             for row, (field, dx, dy) in enumerate(corner_cells):
                 x = ex - dx if side == 0 else ex + X - 1 + dx
                 y = fy + Y - 1 + dy if high else fy - dy
-                line = ref[3 * cx + side, pl.ds(row, 1), :]
+                line = ref[deep + side, pl.ds(row, 1), :]
                 if field == 3:
                     step[x, pl.ds(y, 1), :] = line
                 else:
                     force[field, x, pl.ds(y, 1), :] = line
 
-    def move(old, new, x, components, start, size):
+    pair_sum, pair_gap = neighbour_matrices(Z, 1)
+
+    def move(old, new, x, count, components, start, size):
         rows, above, below = pl.ds(ey + start, size), pl.ds(ey + start + 1, size), pl.ds(ey + start - 1, size)
         source_rows = pl.ds(fy + start, size)
-        ratio = step[x, source_rows, :]
-        for a in components:
+        planes, right, left = pl.ds(x, count), pl.ds(x + 1, count), pl.ds(x - 1, count)
+        shape = (count, size, Z)
+        ratio = step[planes, source_rows, :]
+        middles = [old[a, planes, rows, :] for a in components]
+        sums = apply(pair_sum, jnp.concatenate([flat(v) for v in middles], 0))
+        for number, a in enumerate(components):
             if a == 0:
-                slope = state[3, x + 1, rows, :] - state[3, x - 1, rows, :]
+                slope = state[3, right, rows, :] - state[3, left, rows, :]
             elif a == 1:
-                slope = state[3, x, above, :] - state[3, x, below, :]
+                slope = state[3, planes, above, :] - state[3, planes, below, :]
+            elif 0:
+                slope = apply(pair_gap, flat(state[3, planes, rows, :])).reshape(shape)
             else:
-                press = state[3, x, rows, :]
+                press = state[3, planes, rows, :]
                 slope = roll(press, -1) - roll(press, 1)
-            middle = old[a, x, rows, :]
-            near = old[a, x + 1, rows, :] + old[a, x - 1, rows, :]
-            near = near + (old[a, x, above, :] + old[a, x, below, :])
-            near = near + (roll(middle, 1) + roll(middle, -1))
-            source = force[a, x, source_rows, :]
+            near = old[a, right, rows, :] + old[a, left, rows, :]
+            near = near + (old[a, planes, above, :] + old[a, planes, below, :])
+            near = near + sums[number * count * size : (number + 1) * count * size].reshape(shape)
+            source = force[a, planes, source_rows, :]
             if a == 0:
                 source = source + mean_drive
             source = source - 0.5 * slope + near
-            new[a, x, rows, :] = keep * middle + ratio * source
-
-    def divergence(vel, x, start, size):
+            new[a, planes, rows, :] = keep * middles[number] + ratio * source
+
+    def divergence(vel, x, count, start, size):
         rows, above, below = pl.ds(ey + start, size), pl.ds(ey + start + 1, size), pl.ds(ey + start - 1, size)
-        along_z = vel[2, x, rows, :]
-        total = (vel[0, x + 1, rows, :] - vel[0, x - 1, rows, :]) + (vel[1, x, above, :] - vel[1, x, below, :])
-        return (total + (roll(along_z, -1) - roll(along_z, 1))) * (0.5 * pressure_step)
-
-    def loop(low, high, body):
-        def run(x, carry):
-            body(x)
+        planes, right, left = pl.ds(x, count), pl.ds(x + 1, count), pl.ds(x - 1, count)
+        total = (vel[0, right, rows, :] - vel[0, left, rows, :]) + (vel[1, planes, above, :] - vel[1, planes, below, :])
+        along_z = vel[2, planes, rows, :]
+        if 1:
+            total = total + apply(pair_gap, flat(along_z)).reshape(total.shape)
+        else:
+            total = total + (roll(along_z, -1) - roll(along_z, 1))
+        return total * (0.5 * pressure_step)
+
+    def loop(low, high, most, body):
+        count = max(n for n in range(1, most + 1) if (high - low) % n == 0)
+
+        def run(number, carry):
+            body(low + number * count, count)
             return carry
 
-        lax.fori_loop(low, high, run, 0, unroll=10)
-
-    loop(1, X + 7, lambda x: move(state, mid, x, (0, 1, 2), -8, wide))
-
-    def press_first(x):
-        state[3, x, wide_rows, :] = state[3, x, wide_rows, :] - divergence(mid, x, -8, wide)
-
-    loop(2, X + 6, press_first)
-    move(mid, state, ex - 1, (0,), 0, Y)
-    move(mid, state, ex + X, (0,), 0, Y)
-
-    def second_move(x):
-        move(mid, state, x, (0, 2), 0, Y)
-        move(mid, state, x, (1,), -8, wide)
-
-    loop(ex, ex + X, second_move)
+        lax.fori_loop(0, (high - low) // count, run, 0)
+
+    loop(1, X + 7, 30, lambda x, count: move(state, mid, x, count, (0, 1, 2), -8, wide))
+
+    def press_first(x, count):
+        planes = pl.ds(x, count)
+        state[3, planes, wide_rows, :] = state[3, planes, wide_rows, :] - divergence(mid, x, count, -8, wide)
+
+    loop(2, X + 6, 28, press_first)
+    move(mid, state, ex - 1, 1, (0,), 0, Y)
+    move(mid, state, ex + X, 1, (0,), 0, Y)
+
+    def second_move(x, count):
+        move(mid, state, x, count, (0, 2), 0, Y)
+        move(mid, state, x, count, (1,), -8, wide)
+
+    loop(ex, ex + X, 24, second_move)
     inner = pl.ds(ey, Y)
     last = [copy(state.at[a, pl.ds(ex, X), inner, :], velo_out.at[a]) for a in range(3)]
 
-    def press_second(x):
-        mask_rows = state[3, x, inner, :] - divergence(state, x, 0, Y)
-        step[x, pl.ds(fy, Y), :] = mask_rows
-
-    loop(ex, ex + X, press_second)
+    def press_second(x, count):
+        planes = pl.ds(x, count)
+        step[planes, pl.ds(fy, Y), :] = state[3, planes, inner, :] - divergence(state, x, count, 0, Y)
+
+    loop(ex, ex + X, 24, press_second)
     last.append(copy(step.at[pl.ds(ex, X), pl.ds(fy, Y), :], press_out))
     for made in last:
         made.wait()
 
 
 def relay_kernel(sizes, ml_ref, mp_ref, mr_ref, yp_ref, ym_ref, up_ref, down_ref):
-    X, Y, Z = sizes
-    cx = X // 4
+    cx = sizes[0] // 4
     for ref, lines, corner in ((down_ref, yp_ref, cx), (up_ref, ym_ref, cx + 1)):
-        for number, source in enumerate((ml_ref, mp_ref, mr_ref)):
-            ref[pl.ds(number * cx, cx)] = source[pl.ds(0, cx)]
-        ref[3 * cx] = ml_ref[corner]
-        ref[3 * cx + 1] = mr_ref[corner]
-        ref[pl.ds(3 * cx + 2, 10 * X // 8)] = lines[...]
+        ref[pl.ds(0, 5)] = ml_ref[pl.ds(cx - 5, 5)]
+        ref[pl.ds(5, cx)] = mp_ref[pl.ds(0, cx)]
+        ref[pl.ds(5 + cx, 5)] = mr_ref[pl.ds(0, 5)]
+        ref[cx + 10] = ml_ref[corner]
+        ref[cx + 11] = mr_ref[corner]
+        ref[pl.ds(cx + 12, lines.shape[0])] = lines[...]
 
 
 def shift(value, axis, by):
@@ -344,7 +385,7 @@
     xr = shift(xm, "grp", -1)
     ml = shift(mp, "grp", 1)
     mr = shift(mm, "grp", -1)
-    joined = made((3 * cx + 2 + 10 * X // 8, 8, Z), f32)
+    joined = made((cx + 12 + 10 * X // 8, 8, Z), f32)
     to_up, to_down = pl.pallas_call(
         functools.partial(relay_kernel, sizes),
         out_shape=(joined, joined),
@@ -353,22 +394,30 @@
         compiler_params=pltpu.CompilerParams(vmem_limit_bytes=2 * 2**20),
         name="relay",
     )(ml, mp, mr, yp, ym)
+    down = shift(to_down, "dev", 1)
     up = shift(to_up, "dev", -1)
-    down = shift(to_down, "dev", 1)
-    tall = 3 * cy
+    tall, deep = 3 * cy, cx + 10
+    yfine = pl.pallas_call(
+        functools.partial(coarse_kernel, sizes),
+        out_shape=made((4, cx + 4, Y + 16, Z), f32),
+        in_specs=[near] * 5,
+        out_specs=near,
+        scratch_shapes=[
+            vmem((3, deep, tall, Z), f32),
+            vmem((deep, tall, Z), f32),
+            vmem((2, 3, deep, tall + 2 * cy, Z), f32),
+            vmem((deep, tall + 2 * cy, Z), f32),
+            vmem((4, cx + 4, tall, Z), f32),
+        ],
+        compiler_params=pltpu.CompilerParams(vmem_limit_bytes=16 * 2**20),
+        name="coarse",
+    )(down, up, ml, mp, mr)
     return pl.pallas_call(
         functools.partial(solve_kernel, sizes),
         out_shape=(made((3, X, Y, Z), f32), made((X, Y, Z), f32)),
-        in_specs=[near] * 9,
+        in_specs=[near] * 7,
         out_specs=(anywhere, anywhere),
         scratch_shapes=[
-            vmem((3, 3 * cx, tall, Z), f32),
-            vmem((3 * cx, tall, Z), f32),
-            vmem((3, 3 * cx, tall + 2 * cy, Z), f32),
-            vmem((3, 3 * cx, tall + 2 * cy, Z), f32),
-            vmem((3 * cx, tall + 2 * cy, Z), f32),
-            vmem((4, cx + 4, tall, Z), f32),
-            vmem((4, cx + 4, Y + 16, Z), f32),
             vmem((3, X + 8, Y + 16, Z), f32),
             vmem((X + 8, Y + 16, Z), f32),
             vmem((4, X + 8, Y + 32, Z), f32),
@@ -377,7 +426,7 @@
         ],
         compiler_params=pltpu.CompilerParams(vmem_limit_bytes=32 * 2**20),
         name="solve",
-    )(down, up, ml, mp, mr, xl, xr, mask.reshape(X, Y, Z), force.reshape(3, X, Y, Z))
+    )(yfine, down, up, xl, xr, mask.reshape(X, Y, Z), force.reshape(3, X, Y, Z))
 
 
 def solution(mesh):

time: 28.5 us -> 25.3 us (0.89)
  Pallas kernels: 10.4 us -> 7.44 us
  waiting for transfers between devices: 8.41 us -> 8.07 us
    pallas_call x1, Pallas kernels: 8.51 us -> 4.5 us  [shards(): pl.pallas_call(functools.partial(solve_kernel, sizes), out_shape=(made((3...]
    pallas_call x0 -> x1, Pallas kernels: none -> 1.09 us  [shards(): pl.pallas_call(functools.partial(coarse_kernel, sizes), out_shape=made((4...]
    ppermute x6, waiting for transfers between devices: 8.41 us -> 8.07 us  [shift(): lax.ppermute(value, axis, [(i, (i + by) % count) for i in range(count)])]
  transfers between devices with their start and end apart: 6 -> 6, of which waited for: 4 -> 4; matrix products, arithmetic and copies ran while one was open for 0% -> 0% of each run, Pallas kernels for 0% -> 4%
where the time goes in v3:
time: 25.3 us; the launch traced here: 25.1 us
  starting transfers between devices  8.95 us (35%)
  waiting for transfers between devices  8.07 us (32%)
  Pallas kernels  7.44 us (29%)
  between operations  0.67 us (3%)
    ppermute x6, starting transfers between devices, shift(): lax.ppermute(value, axis, [(i, (i + by) % count) for i in range(count)])  8.95 us
    ppermute x6, waiting for transfers between devices, shift(): lax.ppermute(value, axis, [(i, (i + by) % count) for i in range(count)])  8.07 us
    pallas_call x1, Pallas kernels, shards(): pl.pallas_call(functools.partial(solve_kernel, sizes), out_shape=(made((3...  4.5 us
    pallas_call x1, Pallas kernels, shards(): pl.pallas_call(functools.partial(pack_kernel, sizes), out_shape=(message,...  1.83 us
    pallas_call x1, Pallas kernels, shards(): pl.pallas_call(functools.partial(coarse_kernel, sizes), out_shape=made((4...  1.09 us
  transfers between devices with their start and end apart: 6, of which 4 were waited for; matrix products, arithmetic and copies ran while one was open for 0% of the time, Pallas kernels for 4%

profile of v3, /device:TPU:0, one launch (start us, length us, event | category | flops | bytes accessed | tf_op | source)
XLA Modules:
  0.0 25.1 jit_solution(14971193821922858991)
XLA Ops:
  0.6 1.8 %pack.1 = (f32[8,8,128]{2,1,0:T(8,128)S(1)}, f32[8,8,128]{2,1,0:T(8,128)S(1)}, f32[10,32,128]{2,1,0:T(8,128)S(1)}, f32[10,32,128]{2,1,0:T(8,128)S(1)}, f32[30,8,...) custom-call(s32[768,128]{1,0:T(8,128)} %bitcast.7, ...), custom_call_target="tpu_custom_call" | custom-call | tf_op jit(solution)/shard_map/pack/pallas_call | solution.py:372
  2.5 2.4 %collective-permute-start.1 = (f32[8,8,128]{2,1,0:T(8,128)S(1)}, f32[8,8,128]{2,1,0:T(8,128)S(1)}, u32[]{:S(2)}, u32[]{:S(2)}) collective-permute-start(f32[8,8,128]{2,1,0:T(8,128)S(1)} %get-tuple-element.13), channel_id=1, source_target_pairs={{0,24},{8,0},{16,8},{24,16},{1,25},{9,1},{17,9},{25,17},{2,26},{10... | collective-permute-start | bytes 98312 | tf_op jit(solution)/shard_map/ppermute | solution.py:358
  4.9 0.0 collective-permute-start
  4.9 1.7 %collective-permute-done.1.mr_ref = f32[8,8,128]{2,1,0:T(8,128)S(1)} collective-permute-done((f32[8,8,128]{2,1,0:T(8,128)S(1)}, f32[8,8,128]{2,1,0:T(8,128)S(1)}, u32[]{:S(2)}, u32[]{:S(2)}) %collective-permute-start.1) | collective-permute-done | bytes 32800 | tf_op jit(solution)/shard_map/ppermute | solution.py:358
  6.6 1.6 %collective-permute-done.ml_ref = f32[8,8,128]{2,1,0:T(8,128)S(1)} collective-permute-done((f32[8,8,128]{2,1,0:T(8,128)S(1)}, f32[8,8,128]{2,1,0:T(8,128)S(1)}, u32[]{:S(2)}, u32[]{:S(2)}) %collective-permute-start) | collective-permute-done | bytes 32800 | tf_op jit(solution)/shard_map/ppermute | solution.py:358
  8.3 1.6 %collective-permute-start.2 = (f32[48,8,128]{2,1,0:T(8,128)S(1)}, f32[48,8,128]{2,1,0:T(8,128)S(1)}, u32[]{:S(2)}, u32[]{:S(2)}) collective-permute-start(f32[48,8,128]{2,1,0:T(8,128)S(1)} %get-tuple-element.16), channel_id=1, source_target_pairs={{0,1},{1,2},{2,3},{3,4},{4,5},{5,6},{6,7},{7,0},{8,9},{9,10},{10,1... | collective-permute-start | bytes 589832 | tf_op jit(solution)/shard_map/ppermute | solution.py:358
  9.8 3.2 %collective-permute-start.3 = (f32[48,8,128]{2,1,0:T(8,128)S(1)}, f32[48,8,128]{2,1,0:T(8,128)S(1)}, u32[]{:S(2)}, u32[]{:S(2)}) collective-permute-start(f32[48,8,128]{2,1,0:T(8,128)S(1)} %get-tuple-element.17), channel_id=1, source_target_pairs={{0,7},{1,0},{2,1},{3,2},{4,3},{5,4},{6,5},{7,6},{8,15},{9,8},{10,9... | collective-permute-start | bytes 589832 | tf_op jit(solution)/shard_map/ppermute | solution.py:358
  13.0 0.0 collective-permute-start.4
  13.0 1.7 %collective-permute-start.5 = (f32[10,32,128]{2,1,0:T(8,128)S(1)}, f32[10,32,128]{2,1,0:T(8,128)S(1)}, u32[]{:S(2)}, u32[]{:S(2)}) collective-permute-start(f32[10,32,128]{2,1,0:T(8,128)S(1)} %get-tuple-element.19), channel_id=1, source_target_pairs={{0,24},{8,0},{16,8},{24,16},{1,25},{9,1},{17,9},{25,17},{2,26},{10... | collective-permute-start | bytes 491528 | tf_op jit(solution)/shard_map/ppermute | solution.py:358
  14.8 2.5 %collective-permute-done.2.down_ref.refs_1_ = f32[48,8,128]{2,1,0:T(8,128)S(1)} collective-permute-done((f32[48,8,128]{2,1,0:T(8,128)S(1)}, f32[48,8,128]{2,1,0:T(8,128)S(1)}, u32[]{:S(2)}, u32[]{:S(2)}) %collective-permute-start.2) | collective-permute-done | bytes 196640 | tf_op jit(solution)/shard_map/ppermute | solution.py:358
  17.3 2.2 %collective-permute-done.3.up_ref.refs_2_ = f32[48,8,128]{2,1,0:T(8,128)S(1)} collective-permute-done((f32[48,8,128]{2,1,0:T(8,128)S(1)}, f32[48,8,128]{2,1,0:T(8,128)S(1)}, u32[]{:S(2)}, u32[]{:S(2)}) %collective-permute-start.3) | collective-permute-done | bytes 196640 | tf_op jit(solution)/shard_map/ppermute | solution.py:358
  19.5 1.1 %coarse.1.refs_0_ = f32[4,10,48,128]{3,2,1,0:T(8,128)S(1)} custom-call(f32[48,8,128]{2,1,0:T(8,128)S(1)} %collective-permute-done.2.down_ref.refs_1_, f32[48,8,128]{2,1,0:T(8,128)S(1)} %collective-permute-done.3.up_ref.refs_2_, f32[8,8,128]{2,1,0:T(8,128)S(1)} %collective-permute-done.ml_ref, f32[8,8,128]{2,1,0:T(8,128)S(1)} %get-tuple-element.12.mp_ref, ...), custom_call_target="tpu_custom_call" | custom-call | tf_op jit(solution)/shard_map/coarse/pallas_call | solution.py:400
  20.6 0.0 collective-permute-done.4.refs_3_
  20.6 0.0 collective-permute-done.5.refs_4_
  20.6 4.5 %solve.1 = (f32[3,24,32,128]{3,2,1,0:T(8,128)}, f32[24,32,128]{2,1,0:T(8,128)}) custom-call(f32[4,10,48,128]{3,2,1,0:T(8,128)S(1)} %coarse.1.refs_0_, f32[48,8,128]{2,1,0:T(8,128)S(1)} %collective-permute-done.2.down_ref.refs_1_, f32[48,8,128]{2,1,0:T(8,128)S(1)} %collective-permute-done.3.up_ref.refs_2_, f32[10,32,128]{2,1,0:T(8,128)S(1)} %collective-permute-done.4.refs_3_, ...), custom_call_target="tpu_custom_call" | custom-call | tf_op jit(solution)/shard_map/solve/pallas_call | solution.py:415
  (1 shorter events, 0.0 us)
Async XLA Ops:
  2.5 4.2 %collective-permute-start.1 = (f32[8,8,128]{2,1,0:T(8,128)S(1)}, f32[8,8,128]{2,1,0:T(8,128)S(1)}, u32[]{:S(2)}, u32[]{:S(2)}) collective-permute-start(f32[8,8,128]{2,1,0:T(8,128)S(1)} %get-tuple-element.13), channel_id=1, source_target_pairs={{0,24},{8,0},{16,8},{24,16},{1,25},{9,1},{17,9},{25,17},{2,26},{10... | collective-permute-start | bytes 98312 | tf_op jit(solution)/shard_map/ppermute | solution.py:358
  4.9 3.3 %collective-permute-start = (f32[8,8,128]{2,1,0:T(8,128)S(1)}, f32[8,8,128]{2,1,0:T(8,128)S(1)}, u32[]{:S(2)}, u32[]{:S(2)}) collective-permute-start(f32[8,8,128]{2,1,0:T(8,128)S(1)} %get-tuple-element.12.mp_ref), channel_id=1, source_target_pairs={{0,8},{8,16},{16,24},{24,0},{1,9},{9,17},{17,25},{25,1},{2,10},{10... | collective-permute-start | bytes 98312 | tf_op jit(solution)/shard_map/ppermute | solution.py:358
  8.3 9.1 %collective-permute-start.2 = (f32[48,8,128]{2,1,0:T(8,128)S(1)}, f32[48,8,128]{2,1,0:T(8,128)S(1)}, u32[]{:S(2)}, u32[]{:S(2)}) collective-permute-start(f32[48,8,128]{2,1,0:T(8,128)S(1)} %get-tuple-element.16), channel_id=1, source_target_pairs={{0,1},{1,2},{2,3},{3,4},{4,5},{5,6},{6,7},{7,0},{8,9},{9,10},{10,1... | collective-permute-start | bytes 589832 | tf_op jit(solution)/shard_map/ppermute | solution.py:358
  9.8 9.7 %collective-permute-start.3 = (f32[48,8,128]{2,1,0:T(8,128)S(1)}, f32[48,8,128]{2,1,0:T(8,128)S(1)}, u32[]{:S(2)}, u32[]{:S(2)}) collective-permute-start(f32[48,8,128]{2,1,0:T(8,128)S(1)} %get-tuple-element.17), channel_id=1, source_target_pairs={{0,7},{1,0},{2,1},{3,2},{4,3},{5,4},{6,5},{7,6},{8,15},{9,8},{10,9... | collective-permute-start | bytes 589832 | tf_op jit(solution)/shard_map/ppermute | solution.py:358
  13.0 7.6 %collective-permute-start.4 = (f32[10,32,128]{2,1,0:T(8,128)S(1)}, f32[10,32,128]{2,1,0:T(8,128)S(1)}, u32[]{:S(2)}, u32[]{:S(2)}) collective-permute-start(f32[10,32,128]{2,1,0:T(8,128)S(1)} %get-tuple-element.18), channel_id=1, source_target_pairs={{0,8},{8,16},{16,24},{24,0},{1,9},{9,17},{17,25},{25,1},{2,10},{10... | collective-permute-start | bytes 491528 | tf_op jit(solution)/shard_map/ppermute | solution.py:358
  13.0 7.6 %collective-permute-start.5 = (f32[10,32,128]{2,1,0:T(8,128)S(1)}, f32[10,32,128]{2,1,0:T(8,128)S(1)}, u32[]{:S(2)}, u32[]{:S(2)}) collective-permute-start(f32[10,32,128]{2,1,0:T(8,128)S(1)} %get-tuple-element.19), channel_id=1, source_target_pairs={{0,24},{8,0},{16,8},{24,16},{1,25},{9,1},{17,9},{25,17},{2,26},{10... | collective-permute-start | bytes 491528 | tf_op jit(solution)/shard_map/ppermute | solution.py:358

commit v4 on v3

--- a/solution.py
+++ b/solution.py
@@ -52,7 +52,7 @@
     return jnp.where(mask != 0, solid_step, pore_step).astype(jnp.float32)
 
 
-def pack_kernel(sizes, mask_in, force_in, mp_ref, mm_ref, xp_ref, xm_ref, yp_ref, ym_ref, mask_ref, force_ref, sums, sems):
+def pack_kernel(sizes, mask_in, force_in, mp_ref, mm_ref, xp_ref, xm_ref, mask_ref, force_ref, sums, sems):
     X, Y, Z = sizes
     cx, cy = X // 4, Y // 4
     copies = [
@@ -100,13 +100,13 @@
             packed = mean if packed is None else jnp.where(phase == field, mean, packed)
         mp_ref[block] = packed
         mm_ref[block] = packed
-    for ref, high in ((mp_ref, True), (mm_ref, False)):
-        for top in (True, False):
+    for ref, top in ((mp_ref, True), (mm_ref, False)):
+        for high in (True, False):
             for number, (field, dx, dy) in enumerate(corner_cells):
                 x = X - dx if high else dx - 1
                 y = Y - dy if top else dy - 1
-                ref[cx + (0 if top else 1), pl.ds(number, 1), :] = values(field, x * Y + y, 1)
-            ref[cx + (0 if top else 1), pl.ds(7, 1), :] = jnp.zeros((1, Z), jnp.float32)
+                ref[cx + (0 if high else 1), pl.ds(number, 1), :] = values(field, x * Y + y, 1)
+            ref[cx + (0 if high else 1), pl.ds(7, 1), :] = jnp.zeros((1, Z), jnp.float32)
     for ref, high in ((xp_ref, True), (xm_ref, False)):
         number = 0
         for field, depth in x_depths:
@@ -114,18 +114,18 @@
                 x = X - depth + plane if high else plane
                 ref[number] = values(field, x * Y, Y)
                 number += 1
-    for ref, high in ((yp_ref, True), (ym_ref, False)):
+    for ref, high in ((mp_ref, True), (mm_ref, False)):
         number = 0
         for field, depth in y_depths:
             for row in range(depth):
                 y = Y - depth + row if high else row
                 line = values(field, y, X, Y)
                 for tile in range(X // 8):
-                    ref[number * (X // 8) + tile] = line[8 * tile : 8 * tile + 8]
+                    ref[cx + 2 + number * (X // 8) + tile] = line[8 * tile : 8 * tile + 8]
                 number += 1
 
 
-def coarse_kernel(sizes, down_ref, up_ref, ml_ref, mp_ref, mr_ref, yfine, cforce, cstep, cvel, cpress, cfine):
+def coarse_kernel(sizes, left_ref, right_ref, md_ref, mp_ref, mu_ref, yfine, cforce, cstep, cvel, cpress, cfine):
     X, Y, Z = sizes
     cx, cy = X // 4, Y // 4
     tall, deep = 3 * cy, cx + 10
@@ -142,8 +142,11 @@
 
     packed = []
     for x in range(deep):
-        number, plane = divmod(x + cx - 5, cx)
-        packed += [down_ref[x], (ml_ref, mp_ref, mr_ref)[number][plane], up_ref[x]]
+        if 5 <= x < cx + 5:
+            packed += [md_ref[x - 5], mp_ref[x - 5], mu_ref[x - 5]]
+        else:
+            side, plane = (left_ref, x) if x < 5 else (right_ref, x - 5 - cx)
+            packed += [side[plane], side[5 + plane], side[10 + plane]]
     fields = apply(spread, jnp.concatenate(packed, 0))
     shape = (deep, tall, Z)
     ratio = relaxation / (6.0 * viscosity / 16.0 + penalty * fields[:, 3 * Z :].reshape(shape))
@@ -199,9 +202,9 @@
 def solve_kernel(sizes, *refs):
     X, Y, Z = sizes
     cx = X // 4
-    yfine, down_ref, up_ref, xl_ref, xr_ref, mask, force_ref = refs[:7]
-    velo_out, press_out = refs[7:9]
-    force, step, state, mid, sems = refs[9:]
+    yfine, left_ref, right_ref, yd_ref, yu_ref, xl_ref, xr_ref, mask, force_ref = refs[:9]
+    velo_out, press_out = refs[9:11]
+    force, step, state, mid, sems = refs[11:]
     ex, ey, fy = 4, 16, 8
     deep = cx + 10
 
@@ -242,24 +245,24 @@
         made.wait()
     for x in range(X):
         step[ex + x, pl.ds(fy, Y), :] = step_of(mask[x])
-    for ref, high in ((down_ref, False), (up_ref, True)):
+    for ref, high in ((yd_ref, False), (yu_ref, True)):
         number = 0
         for field, depth in y_depths:
             for row in range(depth):
                 y = fy + Y + row if high else fy - depth + row
                 for x in range(X):
                     place = number * X + x
-                    line = ref[deep + 2 + place // 8, pl.ds(place % 8, 1), :]
+                    line = ref[cx + 2 + place // 8, pl.ds(place % 8, 1), :]
                     if field == 3:
                         step[ex + x, pl.ds(y, 1), :] = line
                     else:
                         force[field, ex + x, pl.ds(y, 1), :] = line
                 number += 1
-        for side in range(2):
+        for side, corner_ref in enumerate((left_ref, right_ref)):
             for row, (field, dx, dy) in enumerate(corner_cells):
                 x = ex - dx if side == 0 else ex + X - 1 + dx
                 y = fy + Y - 1 + dy if high else fy - dy
-                line = ref[deep + side, pl.ds(row, 1), :]
+                line = corner_ref[16 if high else 15, pl.ds(row, 1), :]
                 if field == 3:
                     step[x, pl.ds(y, 1), :] = line
                 else:
@@ -342,15 +345,13 @@
         made.wait()
 
 
-def relay_kernel(sizes, ml_ref, mp_ref, mr_ref, yp_ref, ym_ref, up_ref, down_ref):
+def relay_kernel(sizes, mu_ref, mp_ref, md_ref, right_ref, left_ref):
     cx = sizes[0] // 4
-    for ref, lines, corner in ((down_ref, yp_ref, cx), (up_ref, ym_ref, cx + 1)):
-        ref[pl.ds(0, 5)] = ml_ref[pl.ds(cx - 5, 5)]
-        ref[pl.ds(5, cx)] = mp_ref[pl.ds(0, cx)]
-        ref[pl.ds(5 + cx, 5)] = mr_ref[pl.ds(0, 5)]
-        ref[cx + 10] = ml_ref[corner]
-        ref[cx + 11] = mr_ref[corner]
-        ref[pl.ds(cx + 12, lines.shape[0])] = lines[...]
+    for ref, start, corner in ((right_ref, cx - 5, cx), (left_ref, 0, cx + 1)):
+        for number, source in enumerate((md_ref, mp_ref, mu_ref)):
+            ref[pl.ds(5 * number, 5)] = source[pl.ds(start, 5)]
+        ref[15] = md_ref[corner]
+        ref[16] = mu_ref[corner]
 
 
 def shift(value, axis, by):
@@ -366,14 +367,13 @@
     vmem = pltpu.VMEM
     anywhere = pl.BlockSpec(memory_space=pl.ANY)
     near = pl.BlockSpec(memory_space=vmem)
-    message = made((cx + 2, 8, Z), f32)
+    message = made((cx + 2 + 10 * X // 8, 8, Z), f32)
     planes = made((10, Y, Z), f32)
-    lines = made((10 * X // 8, 8, Z), f32)
-    mp, mm, xp, xm, yp, ym, mask, force = pl.pallas_call(
+    mp, mm, xp, xm, mask, force = pl.pallas_call(
         functools.partial(pack_kernel, sizes),
-        out_shape=(message, message, planes, planes, lines, lines, made((X * Y, Z), jnp.int32), made((3 * X * Y, Z), f32)),
+        out_shape=(message, message, planes, planes, made((X * Y, Z), jnp.int32), made((3 * X * Y, Z), f32)),
         in_specs=[pl.BlockSpec(memory_space=pltpu.HBM)] * 2,
-        out_specs=[near] * 8,
+        out_specs=[near] * 6,
         scratch_shapes=[vmem((4, cx, Y, Z), f32), pltpu.SemaphoreType.DMA((4,))],
         compiler_params=pltpu.CompilerParams(vmem_limit_bytes=12 * 2**20),
         name="pack",
@@ -381,21 +381,21 @@
         pltpu.with_memory_space_constraint(solid_mask.reshape(X * Y, Z), pltpu.HBM),
         pltpu.with_memory_space_constraint(forcing.reshape(3 * X * Y, Z), pltpu.HBM),
     )
+    md = shift(mp, "dev", 1)
+    mu = shift(mm, "dev", -1)
     xl = shift(xp, "grp", 1)
     xr = shift(xm, "grp", -1)
-    ml = shift(mp, "grp", 1)
-    mr = shift(mm, "grp", -1)
-    joined = made((cx + 12 + 10 * X // 8, 8, Z), f32)
-    to_up, to_down = pl.pallas_call(
+    joined = made((17, 8, Z), f32)
+    to_right, to_left = pl.pallas_call(
         functools.partial(relay_kernel, sizes),
         out_shape=(joined, joined),
-        in_specs=[near] * 5,
+        in_specs=[near] * 3,
         out_specs=[near] * 2,
         compiler_params=pltpu.CompilerParams(vmem_limit_bytes=2 * 2**20),
         name="relay",
-    )(ml, mp, mr, yp, ym)
-    down = shift(to_down, "dev", 1)
-    up = shift(to_up, "dev", -1)
+    )(mu, mm, md)
+    left = shift(to_right, "grp", 1)
+    right = shift(to_left, "grp", -1)
     tall, deep = 3 * cy, cx + 10
     yfine = pl.pallas_call(
         functools.partial(coarse_kernel, sizes),
@@ -411,11 +411,11 @@
         ],
         compiler_params=pltpu.CompilerParams(vmem_limit_bytes=16 * 2**20),
         name="coarse",
-    )(down, up, ml, mp, mr)
+    )(left, right, md, mm, mu)
     return pl.pallas_call(
         functools.partial(solve_kernel, sizes),
         out_shape=(made((3, X, Y, Z), f32), made((X, Y, Z), f32)),
-        in_specs=[near] * 7,
+        in_specs=[near] * 9,
         out_specs=(anywhere, anywhere),
         scratch_shapes=[
             vmem((3, X + 8, Y + 16, Z), f32),
@@ -426,7 +426,7 @@
         ],
         compiler_params=pltpu.CompilerParams(vmem_limit_bytes=32 * 2**20),
         name="solve",
-    )(yfine, down, up, xl, xr, mask.reshape(X, Y, Z), force.reshape(3, X, Y, Z))
+    )(yfine, left, right, md, mu, xl, xr, mask.reshape(X, Y, Z), force.reshape(3, X, Y, Z))
 
 
 def solution(mesh):

time: 25.3 us -> 25.1 us (level)
  the two profiles are of different devices: /device:TPU:0 before, /device:TPU:1 now
where the time goes in v4:
time: 25.1 us; the launch traced here: 25 us
  starting transfers between devices  10.4 us (41%)
  Pallas kernels  7.55 us (30%)
  waiting for transfers between devices  6.39 us (25%)
  between operations  0.67 us (3%)
    ppermute x6, starting transfers between devices, shift(): lax.ppermute(value, axis, [(i, (i + by) % count) for i in range(count)])  10.4 us
    ppermute x6, waiting for transfers between devices, shift(): lax.ppermute(value, axis, [(i, (i + by) % count) for i in range(count)])  6.39 us
    pallas_call x1, Pallas kernels, shards(): pl.pallas_call(functools.partial(solve_kernel, sizes), out_shape=(made((3...  4.61 us
    pallas_call x1, Pallas kernels, shards(): pl.pallas_call(functools.partial(pack_kernel, sizes), out_shape=(message,...  1.83 us
    pallas_call x1, Pallas kernels, shards(): pl.pallas_call(functools.partial(coarse_kernel, sizes), out_shape=made((4...  1.09 us
  transfers between devices with their start and end apart: 6, of which 4 were waited for; matrix products, arithmetic and copies ran while one was open for 0% of the time, Pallas kernels for 4%

profile of v4, /device:TPU:1, one launch (start us, length us, event | category | flops | bytes accessed | tf_op | source)
XLA Modules:
  0.0 25.0 jit_solution(3085011536477213168)
XLA Ops:
  0.6 1.8 %pack.1 = (f32[38,8,128]{2,1,0:T(8,128)S(1)}, f32[38,8,128]{2,1,0:T(8,128)S(1)}, f32[10,32,128]{2,1,0:T(8,128)S(1)}, f32[10,32,128]{2,1,0:T(8,128)S(1)}, s32[768...) custom-call(s32[768,128]{1,0:T(8,128)} %bitcast.7, f32[2304,128]{1,0:T(8,128)} %bitcast.6), custom_call_target="tpu_custom_call" | custom-call | tf_op jit(solution)/shard_map/pack/pallas_call | solution.py:372
  2.5 2.1 %collective-permute-start.1 = (f32[38,8,128]{2,1,0:T(8,128)S(1)}, f32[38,8,128]{2,1,0:T(8,128)S(1)}, u32[]{:S(2)}, u32[]{:S(2)}) collective-permute-start(f32[38,8,128]{2,1,0:T(8,128)S(1)} %get-tuple-element.11), channel_id=1, source_target_pairs={{0,1},{1,2},{2,3},{3,4},{4,5},{5,6},{6,7},{7,0},{8,9},{9,10},{10,1... | collective-permute-start | bytes 466952 | tf_op jit(solution)/shard_map/ppermute | solution.py:359
  4.6 3.1 %collective-permute-start = (f32[38,8,128]{2,1,0:T(8,128)S(1)}, f32[38,8,128]{2,1,0:T(8,128)S(1)}, u32[]{:S(2)}, u32[]{:S(2)}) collective-permute-start(f32[38,8,128]{2,1,0:T(8,128)S(1)} %get-tuple-element.10.mp_ref), channel_id=1, source_target_pairs={{0,7},{1,0},{2,1},{3,2},{4,3},{5,4},{6,5},{7,6},{8,15},{9,8},{10,9... | collective-permute-start | bytes 466952 | tf_op jit(solution)/shard_map/ppermute | solution.py:359
  7.7 2.2 %collective-permute-start.4 = (f32[10,32,128]{2,1,0:T(8,128)S(1)}, f32[10,32,128]{2,1,0:T(8,128)S(1)}, u32[]{:S(2)}, u32[]{:S(2)}) collective-permute-start(f32[10,32,128]{2,1,0:T(8,128)S(1)} %get-tuple-element.14), channel_id=1, source_target_pairs={{0,8},{8,16},{16,24},{24,0},{1,9},{9,17},{17,25},{25,1},{2,10},{10... | collective-permute-start | bytes 491528 | tf_op jit(solution)/shard_map/ppermute | solution.py:359
  9.8 0.0 collective-permute-start.5
  9.8 1.5 %collective-permute-done.1.md_ref.refs_3_ = f32[38,8,128]{2,1,0:T(8,128)S(1)} collective-permute-done((f32[38,8,128]{2,1,0:T(8,128)S(1)}, f32[38,8,128]{2,1,0:T(8,128)S(1)}, u32[]{:S(2)}, u32[]{:S(2)}) %collective-permute-start.1) | collective-permute-done | bytes 155680 | tf_op jit(solution)/shard_map/ppermute | solution.py:359
  11.4 1.1 %collective-permute-done.mu_ref.refs_4_ = f32[38,8,128]{2,1,0:T(8,128)S(1)} collective-permute-done((f32[38,8,128]{2,1,0:T(8,128)S(1)}, f32[38,8,128]{2,1,0:T(8,128)S(1)}, u32[]{:S(2)}, u32[]{:S(2)}) %collective-permute-start) | collective-permute-done | bytes 155680 | tf_op jit(solution)/shard_map/ppermute | solution.py:359
  12.5 3.0 %collective-permute-start.2 = (f32[17,8,128]{2,1,0:T(8,128)S(1)}, f32[17,8,128]{2,1,0:T(8,128)S(1)}, u32[]{:S(2)}, u32[]{:S(2)}) collective-permute-start(f32[17,8,128]{2,1,0:T(8,128)S(1)} %get-tuple-element.12), channel_id=1, source_target_pairs={{0,8},{8,16},{16,24},{24,0},{1,9},{9,17},{17,25},{25,1},{2,10},{10... | collective-permute-start | bytes 208904 | tf_op jit(solution)/shard_map/ppermute | solution.py:359
  15.5 0.0 collective-permute-start.3
  15.5 1.4 %collective-permute-done.2.left_ref.refs_1_ = f32[17,8,128]{2,1,0:T(8,128)S(1)} collective-permute-done((f32[17,8,128]{2,1,0:T(8,128)S(1)}, f32[17,8,128]{2,1,0:T(8,128)S(1)}, u32[]{:S(2)}, u32[]{:S(2)}) %collective-permute-start.2) | collective-permute-done | bytes 69664 | tf_op jit(solution)/shard_map/ppermute | solution.py:359
  16.9 2.4 %collective-permute-done.3.right_ref.refs_2_ = f32[17,8,128]{2,1,0:T(8,128)S(1)} collective-permute-done((f32[17,8,128]{2,1,0:T(8,128)S(1)}, f32[17,8,128]{2,1,0:T(8,128)S(1)}, u32[]{:S(2)}, u32[]{:S(2)}) %collective-permute-start.3) | collective-permute-done | bytes 69664 | tf_op jit(solution)/shard_map/ppermute | solution.py:359
  19.3 1.1 %coarse.1.refs_0_ = f32[4,10,48,128]{3,2,1,0:T(8,128)S(1)} custom-call(f32[17,8,128]{2,1,0:T(8,128)S(1)} %collective-permute-done.2.left_ref.refs_1_, f32[17,8,128]{2,1,0:T(8,128)S(1)} %collective-permute-done.3.right_ref.refs_2_, f32[38,8,128]{2,1,0:T(8,128)S(1)} %collective-permute-done.1.md_ref.refs_3_, f32[38,8,128]{2,1,0:T(8,128)S(1)} %get-tuple-element.10.mp_ref, ...), custom_call_target="tpu_custom_call" | custom-call | tf_op jit(solution)/shard_map/coarse/pallas_call | solution.py:400
  20.4 0.0 collective-permute-done.4.refs_5_
  20.4 0.0 collective-permute-done.5.refs_6_
  20.4 4.6 %solve.1 = (f32[3,24,32,128]{3,2,1,0:T(8,128)}, f32[24,32,128]{2,1,0:T(8,128)}) custom-call(f32[4,10,48,128]{3,2,1,0:T(8,128)S(1)} %coarse.1.refs_0_, f32[17,8,128]{2,1,0:T(8,128)S(1)} %collective-permute-done.2.left_ref.refs_1_, f32[17,8,128]{2,1,0:T(8,128)S(1)} %collective-permute-done.3.right_ref.refs_2_, ...), custom_call_target="tpu_custom_call" | custom-call | tf_op jit(solution)/shard_map/solve/pallas_call | solution.py:415
  (1 shorter events, 0.0 us)
Async XLA Ops:
  2.5 8.9 %collective-permute-start.1 = (f32[38,8,128]{2,1,0:T(8,128)S(1)}, f32[38,8,128]{2,1,0:T(8,128)S(1)}, u32[]{:S(2)}, u32[]{:S(2)}) collective-permute-start(f32[38,8,128]{2,1,0:T(8,128)S(1)} %get-tuple-element.11), channel_id=1, source_target_pairs={{0,1},{1,2},{2,3},{3,4},{4,5},{5,6},{6,7},{7,0},{8,9},{9,10},{10,1... | collective-permute-start | bytes 466952 | tf_op jit(solution)/shard_map/ppermute | solution.py:359
  4.6 7.9 %collective-permute-start = (f32[38,8,128]{2,1,0:T(8,128)S(1)}, f32[38,8,128]{2,1,0:T(8,128)S(1)}, u32[]{:S(2)}, u32[]{:S(2)}) collective-permute-start(f32[38,8,128]{2,1,0:T(8,128)S(1)} %get-tuple-element.10.mp_ref), channel_id=1, source_target_pairs={{0,7},{1,0},{2,1},{3,2},{4,3},{5,4},{6,5},{7,6},{8,15},{9,8},{10,9... | collective-permute-start | bytes 466952 | tf_op jit(solution)/shard_map/ppermute | solution.py:359
  7.7 12.7 %collective-permute-start.4 = (f32[10,32,128]{2,1,0:T(8,128)S(1)}, f32[10,32,128]{2,1,0:T(8,128)S(1)}, u32[]{:S(2)}, u32[]{:S(2)}) collective-permute-start(f32[10,32,128]{2,1,0:T(8,128)S(1)} %get-tuple-element.14), channel_id=1, source_target_pairs={{0,8},{8,16},{16,24},{24,0},{1,9},{9,17},{17,25},{25,1},{2,10},{10... | collective-permute-start | bytes 491528 | tf_op jit(solution)/shard_map/ppermute | solution.py:359
  9.8 10.5 %collective-permute-start.5 = (f32[10,32,128]{2,1,0:T(8,128)S(1)}, f32[10,32,128]{2,1,0:T(8,128)S(1)}, u32[]{:S(2)}, u32[]{:S(2)}) collective-permute-start(f32[10,32,128]{2,1,0:T(8,128)S(1)} %get-tuple-element.15), channel_id=1, source_target_pairs={{0,24},{8,0},{16,8},{24,16},{1,25},{9,1},{17,9},{25,17},{2,26},{10... | collective-permute-start | bytes 491528 | tf_op jit(solution)/shard_map/ppermute | solution.py:359
  12.5 4.4 %collective-permute-start.2 = (f32[17,8,128]{2,1,0:T(8,128)S(1)}, f32[17,8,128]{2,1,0:T(8,128)S(1)}, u32[]{:S(2)}, u32[]{:S(2)}) collective-permute-start(f32[17,8,128]{2,1,0:T(8,128)S(1)} %get-tuple-element.12), channel_id=1, source_target_pairs={{0,8},{8,16},{16,24},{24,0},{1,9},{9,17},{17,25},{25,1},{2,10},{10... | collective-permute-start | bytes 208904 | tf_op jit(solution)/shard_map/ppermute | solution.py:359
  15.5 3.7 %collective-permute-start.3 = (f32[17,8,128]{2,1,0:T(8,128)S(1)}, f32[17,8,128]{2,1,0:T(8,128)S(1)}, u32[]{:S(2)}, u32[]{:S(2)}) collective-permute-start(f32[17,8,128]{2,1,0:T(8,128)S(1)} %get-tuple-element.13), channel_id=1, source_target_pairs={{0,24},{8,0},{16,8},{24,16},{1,25},{9,1},{17,9},{25,17},{2,26},{10... | collective-permute-start | bytes 208904 | tf_op jit(solution)/shard_map/ppermute | solution.py:359

commit v5 on v4

--- a/solution.py
+++ b/solution.py
@@ -52,7 +52,7 @@
     return jnp.where(mask != 0, solid_step, pore_step).astype(jnp.float32)
 
 
-def pack_kernel(sizes, mask_in, force_in, mp_ref, mm_ref, xp_ref, xm_ref, mask_ref, force_ref, sums, sems):
+def pack_kernel(sizes, mask_in, force_in, own_ref, mp_ref, mm_ref, xp_ref, xm_ref, mask_ref, force_ref, sums, sems):
     X, Y, Z = sizes
     cx, cy = X // 4, Y // 4
     copies = [
@@ -98,15 +98,19 @@
             if field == 0:
                 mean = mean + mean_drive
             packed = mean if packed is None else jnp.where(phase == field, mean, packed)
-        mp_ref[block] = packed
-        mm_ref[block] = packed
+        own_ref[block] = packed
+        mp_ref.reshape(-1, Z)[pl.ds(5 * block, 5), :] = packed[cy - 5 :]
+        mm_ref.reshape(-1, Z)[pl.ds(5 * block, 5), :] = packed[:5]
+    own_tiles = -(-5 * cx // 8)
+    for ref in (mp_ref, mm_ref):
+        ref.reshape(-1, Z)[pl.ds(5 * cx, 8 * own_tiles - 5 * cx), :] = jnp.zeros((8 * own_tiles - 5 * cx, Z), jnp.float32)
     for ref, top in ((mp_ref, True), (mm_ref, False)):
         for high in (True, False):
             for number, (field, dx, dy) in enumerate(corner_cells):
                 x = X - dx if high else dx - 1
                 y = Y - dy if top else dy - 1
-                ref[cx + (0 if high else 1), pl.ds(number, 1), :] = values(field, x * Y + y, 1)
-            ref[cx + (0 if high else 1), pl.ds(7, 1), :] = jnp.zeros((1, Z), jnp.float32)
+                ref[own_tiles + (0 if high else 1), pl.ds(number, 1), :] = values(field, x * Y + y, 1)
+            ref[own_tiles + (0 if high else 1), pl.ds(7, 1), :] = jnp.zeros((1, Z), jnp.float32)
     for ref, high in ((xp_ref, True), (xm_ref, False)):
         number = 0
         for field, depth in x_depths:
@@ -121,11 +125,11 @@
                 y = Y - depth + row if high else row
                 line = values(field, y, X, Y)
                 for tile in range(X // 8):
-                    ref[cx + 2 + number * (X // 8) + tile] = line[8 * tile : 8 * tile + 8]
+                    ref[own_tiles + 2 + number * (X // 8) + tile] = line[8 * tile : 8 * tile + 8]
                 number += 1
 
 
-def coarse_kernel(sizes, left_ref, right_ref, md_ref, mp_ref, mu_ref, yfine, cforce, cstep, cvel, cpress, cfine):
+def coarse_kernel(sizes, left_ref, right_ref, md_ref, own_ref, low_ref, mu_ref, yfine, gathered, cforce, cstep, cvel, cpress, cfine):
     X, Y, Z = sizes
     cx, cy = X // 4, Y // 4
     tall, deep = 3 * cy, cx + 10
@@ -140,14 +144,23 @@
     stretch = jnp.where(source == (target + Z - 2) % Z, 1.0 - part, 0.0) + jnp.where(source == (target + 2) % Z, part, 0.0)
     stretch = stretch.astype(jnp.bfloat16)
 
-    packed = []
+    far = jnp.zeros((deep, cy - 5, Z), jnp.float32)
+    gathered[:, pl.ds(0, cy - 5), :] = far
+    gathered[:, pl.ds(2 * cy + 5, cy - 5), :] = far
+    below, above = pl.ds(cy - 5, 5), pl.ds(2 * cy, 5)
     for x in range(deep):
         if 5 <= x < cx + 5:
-            packed += [md_ref[x - 5], mp_ref[x - 5], mu_ref[x - 5]]
+            rows = pl.ds(5 * (x - 5), 5)
+            gathered[x, below, :] = md_ref.reshape(-1, Z)[rows, :]
+            gathered[x, pl.ds(cy, 5), :] = low_ref.reshape(-1, Z)[rows, :]
+            gathered[x, pl.ds(cy + 5, cy - 5), :] = own_ref[x - 5, pl.ds(5, cy - 5), :]
+            gathered[x, above, :] = mu_ref.reshape(-1, Z)[rows, :]
         else:
             side, plane = (left_ref, x) if x < 5 else (right_ref, x - 5 - cx)
-            packed += [side[plane], side[5 + plane], side[10 + plane]]
-    fields = apply(spread, jnp.concatenate(packed, 0))
+            gathered[x, below, :] = side[plane, below, :]
+            gathered[x, pl.ds(cy, cy), :] = side[5 + plane]
+            gathered[x, above, :] = side[10 + plane, pl.ds(0, 5), :]
+    fields = apply(spread, flat(gathered[...]))
     shape = (deep, tall, Z)
     ratio = relaxation / (6.0 * viscosity / 16.0 + penalty * fields[:, 3 * Z :].reshape(shape))
     cstep[...] = ratio
@@ -252,7 +265,7 @@
                 y = fy + Y + row if high else fy - depth + row
                 for x in range(X):
                     place = number * X + x
-                    line = ref[cx + 2 + place // 8, pl.ds(place % 8, 1), :]
+                    line = ref[-(-5 * cx // 8) + 2 + place // 8, pl.ds(place % 8, 1), :]
                     if field == 3:
                         step[ex + x, pl.ds(y, 1), :] = line
                     else:
@@ -345,11 +358,18 @@
         made.wait()
 
 
-def relay_kernel(sizes, mu_ref, mp_ref, md_ref, right_ref, left_ref):
-    cx = sizes[0] // 4
-    for ref, start, corner in ((right_ref, cx - 5, cx), (left_ref, 0, cx + 1)):
-        for number, source in enumerate((md_ref, mp_ref, mu_ref)):
-            ref[pl.ds(5 * number, 5)] = source[pl.ds(start, 5)]
+def relay_kernel(sizes, mu_ref, own_ref, md_ref, right_ref, left_ref):
+    cx, cy, Z = sizes[0] // 4, sizes[1] // 4, sizes[2]
+    own_tiles = -(-5 * cx // 8)
+    for ref, start, corner in ((right_ref, cx - 5, own_tiles), (left_ref, 0, own_tiles + 1)):
+        blank = jnp.zeros((5, cy - 5, Z), jnp.float32)
+        ref[pl.ds(0, 5), pl.ds(0, cy - 5), :] = blank
+        ref[pl.ds(10, 5), pl.ds(5, cy - 5), :] = blank
+        for plane in range(5):
+            rows = pl.ds(5 * (start + plane), 5)
+            ref[plane, pl.ds(cy - 5, 5), :] = md_ref.reshape(-1, Z)[rows, :]
+            ref[10 + plane, pl.ds(0, 5), :] = mu_ref.reshape(-1, Z)[rows, :]
+        ref[pl.ds(5, 5)] = own_ref[pl.ds(start, 5)]
         ref[15] = md_ref[corner]
         ref[16] = mu_ref[corner]
 
@@ -367,13 +387,13 @@
     vmem = pltpu.VMEM
     anywhere = pl.BlockSpec(memory_space=pl.ANY)
     near = pl.BlockSpec(memory_space=vmem)
-    message = made((cx + 2 + 10 * X // 8, 8, Z), f32)
+    message = made((-(-5 * cx // 8) + 2 + 10 * X // 8, 8, Z), f32)
     planes = made((10, Y, Z), f32)
-    mp, mm, xp, xm, mask, force = pl.pallas_call(
+    own, mp, mm, xp, xm, mask, force = pl.pallas_call(
         functools.partial(pack_kernel, sizes),
-        out_shape=(message, message, planes, planes, made((X * Y, Z), jnp.int32), made((3 * X * Y, Z), f32)),
+        out_shape=(made((cx, 8, Z), f32), message, message, planes, planes, made((X * Y, Z), jnp.int32), made((3 * X * Y, Z), f32)),
         in_specs=[pl.BlockSpec(memory_space=pltpu.HBM)] * 2,
-        out_specs=[near] * 6,
+        out_specs=[near] * 7,
         scratch_shapes=[vmem((4, cx, Y, Z), f32), pltpu.SemaphoreType.DMA((4,))],
         compiler_params=pltpu.CompilerParams(vmem_limit_bytes=12 * 2**20),
         name="pack",
@@ -393,16 +413,17 @@
         out_specs=[near] * 2,
         compiler_params=pltpu.CompilerParams(vmem_limit_bytes=2 * 2**20),
         name="relay",
-    )(mu, mm, md)
+    )(mu, own, md)
     left = shift(to_right, "grp", 1)
     right = shift(to_left, "grp", -1)
     tall, deep = 3 * cy, cx + 10
     yfine = pl.pallas_call(
         functools.partial(coarse_kernel, sizes),
         out_shape=made((4, cx + 4, Y + 16, Z), f32),
-        in_specs=[near] * 5,
+        in_specs=[near] * 6,
         out_specs=near,
         scratch_shapes=[
+            vmem((deep, tall, Z), f32),
             vmem((3, deep, tall, Z), f32),
             vmem((deep, tall, Z), f32),
             vmem((2, 3, deep, tall + 2 * cy, Z), f32),
@@ -411,7 +432,7 @@
         ],
         compiler_params=pltpu.CompilerParams(vmem_limit_bytes=16 * 2**20),
         name="coarse",
-    )(left, right, md, mm, mu)
+    )(left, right, md, own, mm, mu)
     return pl.pallas_call(
         functools.partial(solve_kernel, sizes),
         out_shape=(made((3, X, Y, Z), f32), made((X, Y, Z), f32)),

time: 25.1 us -> 24.7 us (0.984)
  waiting for transfers between devices: 6.39 us -> 6.04 us
    ppermute x6, waiting for transfers between devices: 6.39 us -> 6.04 us  [shift(): lax.ppermute(value, axis, [(i, (i + by) % count) for i in range(count)])]
  transfers between devices with their start and end apart: 6 -> 6, of which waited for: 4 -> 4; matrix products, arithmetic and copies ran while one was open for 0% -> 0% of each run, Pallas kernels for 4% -> 5%
where the time goes in v5:
time: 24.7 us; the launch traced here: 24.6 us
  starting transfers between devices  10.4 us (42%)
  Pallas kernels  7.49 us (30%)
  waiting for transfers between devices  6.04 us (24%)
  between operations  0.67 us (3%)
    ppermute x6, starting transfers between devices, shift(): lax.ppermute(value, axis, [(i, (i + by) % count) for i in range(count)])  10.4 us
    ppermute x6, waiting for transfers between devices, shift(): lax.ppermute(value, axis, [(i, (i + by) % count) for i in range(count)])  6.04 us
    pallas_call x1, Pallas kernels, shards(): pl.pallas_call(functools.partial(solve_kernel, sizes), out_shape=(made((3...  4.55 us
    pallas_call x1, Pallas kernels, shards(): pl.pallas_call(functools.partial(pack_kernel, sizes), out_shape=(made((cx...  1.83 us
    pallas_call x1, Pallas kernels, shards(): pl.pallas_call(functools.partial(coarse_kernel, sizes), out_shape=made((4...  1.09 us
  transfers between devices with their start and end apart: 6, of which 4 were waited for; matrix products, arithmetic and copies ran while one was open for 0% of the time, Pallas kernels for 5%

profile of v5, /device:TPU:1, one launch (start us, length us, event | category | flops | bytes accessed | tf_op | source)
XLA Modules:
  0.0 24.6 jit_solution(172651852255551027)
XLA Ops:
  0.6 1.8 %pack.1 = (f32[6,8,128]{2,1,0:T(8,128)S(1)}, f32[36,8,128]{2,1,0:T(8,128)S(1)}, f32[36,8,128]{2,1,0:T(8,128)S(1)}, f32[10,32,128]{2,1,0:T(8,128)S(1)}, f32[10,32...) custom-call(s32[768,128]{1,0:T(8,128)} %bitcast.7, f32[2304,128]{1,0:T(8,128)} %bitcast.6), custom_call_target="tpu_custom_call" | custom-call | tf_op jit(solution)/shard_map/pack/pallas_call | solution.py:392
  2.5 2.1 %collective-permute-start.1 = (f32[36,8,128]{2,1,0:T(8,128)S(1)}, f32[36,8,128]{2,1,0:T(8,128)S(1)}, u32[]{:S(2)}, u32[]{:S(2)}) collective-permute-start(f32[36,8,128]{2,1,0:T(8,128)S(1)} %get-tuple-element.13), channel_id=1, source_target_pairs={{0,1},{1,2},{2,3},{3,4},{4,5},{5,6},{6,7},{7,0},{8,9},{9,10},{10,1... | collective-permute-start | bytes 442376 | tf_op jit(solution)/shard_map/ppermute | solution.py:379
  4.6 3.1 %collective-permute-start = (f32[36,8,128]{2,1,0:T(8,128)S(1)}, f32[36,8,128]{2,1,0:T(8,128)S(1)}, u32[]{:S(2)}, u32[]{:S(2)}) collective-permute-start(f32[36,8,128]{2,1,0:T(8,128)S(1)} %get-tuple-element.11.low_ref), channel_id=1, source_target_pairs={{0,7},{1,0},{2,1},{3,2},{4,3},{5,4},{6,5},{7,6},{8,15},{9,8},{10,9... | collective-permute-start | bytes 442376 | tf_op jit(solution)/shard_map/ppermute | solution.py:379
  7.7 2.2 %collective-permute-start.4 = (f32[10,32,128]{2,1,0:T(8,128)S(1)}, f32[10,32,128]{2,1,0:T(8,128)S(1)}, u32[]{:S(2)}, u32[]{:S(2)}) collective-permute-start(f32[10,32,128]{2,1,0:T(8,128)S(1)} %get-tuple-element.16), channel_id=1, source_target_pairs={{0,8},{8,16},{16,24},{24,0},{1,9},{9,17},{17,25},{25,1},{2,10},{10... | collective-permute-start | bytes 491528 | tf_op jit(solution)/shard_map/ppermute | solution.py:379
  9.8 0.0 collective-permute-start.5
  9.8 1.4 %collective-permute-done.1.md_ref.refs_3_ = f32[36,8,128]{2,1,0:T(8,128)S(1)} collective-permute-done((f32[36,8,128]{2,1,0:T(8,128)S(1)}, f32[36,8,128]{2,1,0:T(8,128)S(1)}, u32[]{:S(2)}, u32[]{:S(2)}) %collective-permute-start.1) | collective-permute-done | bytes 147488 | tf_op jit(solution)/shard_map/ppermute | solution.py:379
  11.2 0.9 %collective-permute-done.mu_ref.refs_4_ = f32[36,8,128]{2,1,0:T(8,128)S(1)} collective-permute-done((f32[36,8,128]{2,1,0:T(8,128)S(1)}, f32[36,8,128]{2,1,0:T(8,128)S(1)}, u32[]{:S(2)}, u32[]{:S(2)}) %collective-permute-start) | collective-permute-done | bytes 147488 | tf_op jit(solution)/shard_map/ppermute | solution.py:379
  12.2 3.0 %collective-permute-start.2 = (f32[17,8,128]{2,1,0:T(8,128)S(1)}, f32[17,8,128]{2,1,0:T(8,128)S(1)}, u32[]{:S(2)}, u32[]{:S(2)}) collective-permute-start(f32[17,8,128]{2,1,0:T(8,128)S(1)} %get-tuple-element.14), channel_id=1, source_target_pairs={{0,8},{8,16},{16,24},{24,0},{1,9},{9,17},{17,25},{25,1},{2,10},{10... | collective-permute-start | bytes 208904 | tf_op jit(solution)/shard_map/ppermute | solution.py:379
  15.2 0.0 collective-permute-start.3
  15.2 1.4 %collective-permute-done.2.left_ref.refs_1_ = f32[17,8,128]{2,1,0:T(8,128)S(1)} collective-permute-done((f32[17,8,128]{2,1,0:T(8,128)S(1)}, f32[17,8,128]{2,1,0:T(8,128)S(1)}, u32[]{:S(2)}, u32[]{:S(2)}) %collective-permute-start.2) | collective-permute-done | bytes 69664 | tf_op jit(solution)/shard_map/ppermute | solution.py:379
  16.6 2.4 %collective-permute-done.3.right_ref.refs_2_ = f32[17,8,128]{2,1,0:T(8,128)S(1)} collective-permute-done((f32[17,8,128]{2,1,0:T(8,128)S(1)}, f32[17,8,128]{2,1,0:T(8,128)S(1)}, u32[]{:S(2)}, u32[]{:S(2)}) %collective-permute-start.3) | collective-permute-done | bytes 69664 | tf_op jit(solution)/shard_map/ppermute | solution.py:379
  18.9 1.1 %coarse.1.refs_0_ = f32[4,10,48,128]{3,2,1,0:T(8,128)S(1)} custom-call(f32[17,8,128]{2,1,0:T(8,128)S(1)} %collective-permute-done.2.left_ref.refs_1_, f32[17,8,128]{2,1,0:T(8,128)S(1)} %collective-permute-done.3.right_ref.refs_2_, f32[36,8,128]{2,1,0:T(8,128)S(1)} %collective-permute-done.1.md_ref.refs_3_, f32[6,8,128]{2,1,0:T(8,128)S(1)} %get-tuple-element.12.own_ref, ...), custom_call_target="tpu_custom_call" | custom-call | tf_op jit(solution)/shard_map/coarse/pallas_call | solution.py:420
  20.0 0.0 collective-permute-done.4.refs_5_
  20.0 0.0 collective-permute-done.5.refs_6_
  20.0 4.6 %solve.1 = (f32[3,24,32,128]{3,2,1,0:T(8,128)}, f32[24,32,128]{2,1,0:T(8,128)}) custom-call(f32[4,10,48,128]{3,2,1,0:T(8,128)S(1)} %coarse.1.refs_0_, f32[17,8,128]{2,1,0:T(8,128)S(1)} %collective-permute-done.2.left_ref.refs_1_, f32[17,8,128]{2,1,0:T(8,128)S(1)} %collective-permute-done.3.right_ref.refs_2_, ...), custom_call_target="tpu_custom_call" | custom-call | tf_op jit(solution)/shard_map/solve/pallas_call | solution.py:436
  (1 shorter events, 0.0 us)
Async XLA Ops:
  2.5 8.7 %collective-permute-start.1 = (f32[36,8,128]{2,1,0:T(8,128)S(1)}, f32[36,8,128]{2,1,0:T(8,128)S(1)}, u32[]{:S(2)}, u32[]{:S(2)}) collective-permute-start(f32[36,8,128]{2,1,0:T(8,128)S(1)} %get-tuple-element.13), channel_id=1, source_target_pairs={{0,1},{1,2},{2,3},{3,4},{4,5},{5,6},{6,7},{7,0},{8,9},{9,10},{10,1... | collective-permute-start | bytes 442376 | tf_op jit(solution)/shard_map/ppermute | solution.py:379
  4.6 7.6 %collective-permute-start = (f32[36,8,128]{2,1,0:T(8,128)S(1)}, f32[36,8,128]{2,1,0:T(8,128)S(1)}, u32[]{:S(2)}, u32[]{:S(2)}) collective-permute-start(f32[36,8,128]{2,1,0:T(8,128)S(1)} %get-tuple-element.11.low_ref), channel_id=1, source_target_pairs={{0,7},{1,0},{2,1},{3,2},{4,3},{5,4},{6,5},{7,6},{8,15},{9,8},{10,9... | collective-permute-start | bytes 442376 | tf_op jit(solution)/shard_map/ppermute | solution.py:379
  7.7 12.3 %collective-permute-start.4 = (f32[10,32,128]{2,1,0:T(8,128)S(1)}, f32[10,32,128]{2,1,0:T(8,128)S(1)}, u32[]{:S(2)}, u32[]{:S(2)}) collective-permute-start(f32[10,32,128]{2,1,0:T(8,128)S(1)} %get-tuple-element.16), channel_id=1, source_target_pairs={{0,8},{8,16},{16,24},{24,0},{1,9},{9,17},{17,25},{25,1},{2,10},{10... | collective-permute-start | bytes 491528 | tf_op jit(solution)/shard_map/ppermute | solution.py:379
  9.8 10.2 %collective-permute-start.5 = (f32[10,32,128]{2,1,0:T(8,128)S(1)}, f32[10,32,128]{2,1,0:T(8,128)S(1)}, u32[]{:S(2)}, u32[]{:S(2)}) collective-permute-start(f32[10,32,128]{2,1,0:T(8,128)S(1)} %get-tuple-element.17), channel_id=1, source_target_pairs={{0,24},{8,0},{16,8},{24,16},{1,25},{9,1},{17,9},{25,17},{2,26},{10... | collective-permute-start | bytes 491528 | tf_op jit(solution)/shard_map/ppermute | solution.py:379
  12.2 4.4 %collective-permute-start.2 = (f32[17,8,128]{2,1,0:T(8,128)S(1)}, f32[17,8,128]{2,1,0:T(8,128)S(1)}, u32[]{:S(2)}, u32[]{:S(2)}) collective-permute-start(f32[17,8,128]{2,1,0:T(8,128)S(1)} %get-tuple-element.14), channel_id=1, source_target_pairs={{0,8},{8,16},{16,24},{24,0},{1,9},{9,17},{17,25},{25,1},{2,10},{10... | collective-permute-start | bytes 208904 | tf_op jit(solution)/shard_map/ppermute | solution.py:379
  15.2 3.7 %collective-permute-start.3 = (f32[17,8,128]{2,1,0:T(8,128)S(1)}, f32[17,8,128]{2,1,0:T(8,128)S(1)}, u32[]{:S(2)}, u32[]{:S(2)}) collective-permute-start(f32[17,8,128]{2,1,0:T(8,128)S(1)} %get-tuple-element.15), channel_id=1, source_target_pairs={{0,24},{8,0},{16,8},{24,16},{1,25},{9,1},{17,9},{25,17},{2,26},{10... | collective-permute-start | bytes 208904 | tf_op jit(solution)/shard_map/ppermute | solution.py:379
